TPU v7x, 512 devices: a whole 4x4x16 slice. The times are simulated.
512 devices in a mesh: lat: 64 (over z, x), mem: 8 (over y, core).
Axes of the slice: x: 4, y: 4, z: 16, core: 2. Of those that a mesh axis runs over, the one named last changes fastest.
Arguments:
- field: bfloat16 [8, 64, 128, 2688], P('mem', 'lat'), may hold values from -6 to 6
- lon_count: int32 [64], P('lat'), may hold values from 16 to 2688, as said below
- wave_order: int32 [640], replicated, may hold values from 0 to 639, as said below
- legendre: bfloat16 [640, 64, 640], P('lat'), may hold values from -0.75 to 0.75
Outputs:
- covariance: float32 [2, 320, 128, 128], P(None, 'lat', 'mem')
Inputs may be any that keep to these rules, and one draw needn't show every extreme that they name: `lon_count`: each row's count is 4 k + 16 for a whole k; longitude slots at or beyond it are not part of the row. `wave_order`: each zonal wavenumber stands in exactly one slot; slots 2 t and 2 t + 1 hold wavenumbers that sum to 639.
All inputs are finite; a program needn't handle non-finite values.
Results may differ from a plain program's by a relative error of at most 0.0033.
Values may be sent and summed in bfloat16 or wider, within the bound.
A program may use at most 64 MiB of HBM per device.

v0:
```python
import jax
import jax.numpy as jnp
from jax import lax
from jax.sharding import PartitionSpec as P

TWO_PI = 6.283185307179586


def build_table(wave_order, count, lons):
    column = lax.iota(jnp.int32, lons)
    product = wave_order[:, None] * column[None, :] % count
    angle = product.astype(jnp.float32) * jnp.float32(TWO_PI) / count.astype(jnp.float32)
    inside = (column < count)[None, :]
    real_part = jnp.where(inside, jnp.cos(angle), jnp.float32(0.0))
    imag_part = jnp.where(inside, -jnp.sin(angle), jnp.float32(0.0))
    return jnp.stack([real_part, imag_part], axis=1).astype(jnp.bfloat16)


def per_device(field, lon_count, wave_order, legendre):
    local_members, rows, levels, lons = field.shape
    waves = wave_order.shape[0]
    owned = legendre.shape[0]
    total = legendre.shape[2]
    groups = lax.axis_size("lat")
    half_block = total // (2 * groups)
    own_index = lax.axis_index("lat")
    start = own_index * owned
    owned_waves = lax.dynamic_slice_in_dim(wave_order, start, owned)
    wave_index = lax.iota(jnp.int32, total)
    masked = jnp.where(
        wave_index[None, None, :] >= owned_waves[:, None, None], legendre, jnp.zeros_like(legendre)
    )
    tables = build_table(wave_order, lon_count[0], lons)
    summed = jnp.einsum("mck,lk->mcl", tables, field[0, 0], preferred_element_type=jnp.float32)
    scaled = summed / lon_count[0].astype(jnp.float32)
    pieces = [scaled.astype(jnp.bfloat16).reshape(waves, 2 * levels)]
    fourier = jnp.stack(pieces, axis=1)
    gathered = lax.all_to_all(fourier, "lat", split_axis=0, concat_axis=1, tiled=True)
    spectral = jnp.einsum(
        "srn,srk->snk", masked, gathered, preferred_element_type=jnp.float32
    ).astype(jnp.bfloat16)
    spectral = spectral.reshape(owned, total, 2, levels)
    lower = spectral[:, : total // 2].reshape(owned, groups, half_block, 2, levels)
    upper = jnp.flip(spectral[:, total // 2 :], 1).reshape(owned, groups, half_block, 2, levels)
    folded = jnp.stack([lower, upper], axis=2)
    received = lax.all_to_all(folded, "lat", split_axis=1, concat_axis=0, tiled=True)
    terms = jnp.einsum(
        "sxhica,sxhicb->hiab", received, received, preferred_element_type=jnp.float32
    )
    members = local_members * lax.axis_size("mem")
    whole = lax.psum(terms, "mem")
    count_rows = levels // lax.axis_size("mem")
    summed_rows = lax.dynamic_slice_in_dim(whole, lax.axis_index("mem") * count_rows, count_rows, 2)
    return summed_rows / jnp.float32(members)


def solution(mesh):
    return jax.shard_map(
        per_device,
        mesh=mesh,
        in_specs=(P("mem", "lat", None, None), P("lat"), P(), P("lat", None, None)),
        out_specs=P(None, "lat", "mem", None),
        check_vma=False,
    )
```

profile of v0, /device:TPU:1, one launch (start us, length us, event | category | flops | bytes accessed | tf_op | source)
XLA Modules:
  0.0 414.4 jit_solution(3690146776269058135)
XLA Ops:
  7.3 93.3 %select_convert_fusion.1 = (bf16[640,1,2688]{2,0,1:T(8,128)(2,1)S(1)}, bf16[640,1,2688]{2,0,1:T(8,128)(2,1)S(1)}) fusion(f32[]{:T(128)S(6)} %convert_element_type.26, pred[]{:T(512)S(6)} %lt.39, s32[]{:T(128)S(6)} %select_n.53, s32[640]{0:T(1024)} %param.6, pred[2688]{0:T(1024)(128)(4,1)S(1)} %iota_compare_fusion.1), kind=kLoop, calls=%fused_computation.9 | loop fusion | flops 27525120 | bytes 6886537 | tf_op jit(solution)/shard_map/convert
  100.6 2.0 fusion.19
  102.6 0.5 broadcast.175
  103.2 0.8 reduce.1
  104.0 0.2 copy.35
  104.2 0.9 reshape.166
  105.0 19.1 %all-to-all-start = ((bf16[64,2,1280]{2,1,0:T(2,128)(2,1)}), bf16[64,2,1280]{2,1,0:T(2,128)(2,1)S(1)}, u32[]{:S(2)}, u32[]{:S(2)}) async-start(bf16[64,2,1280]{2,1,0:T(2,128)(2,1)} %reshape.166), calls=%async_computation | async-start | bytes 655360 | tf_op jit(solution)/shard_map/all_to_all | solution.py:38
  124.2 0.8 dynamic_slice.6
  125.0 21.2 %all-to-all-done = bf16[64,2,1280]{2,1,0:T(2,128)(2,1)S(1)} async-done(((bf16[64,2,1280]{2,1,0:T(2,128)(2,1)}), bf16[64,2,1280]{2,1,0:T(2,128)(2,1)S(1)}, u32[]{:S(2)}, u32[]{:S(2)}) %all-to-all-start) | async-done | bytes 327712 | tf_op jit(solution)/shard_map/all_to_all | solution.py:38
  146.2 0.3 reshape.167
  146.5 2.0 reduce
  148.5 0.1 all_to_all.25
  148.6 1.1 convolution_convert_fusion
  149.7 2.5 fusion.30
  152.2 6.6 %copy.26 = bf16[10,320,2,128]{3,2,1,0:T(2,128)(2,1)} copy(bf16[10,320,2,128]{1,3,2,0:T(8,128)(2,1)} %get-tuple-element.6) | data formatting | bytes 3276800
  158.7 3.9 rev.4
  162.7 4.5 %copy.25 = bf16[10,320,2,128]{3,2,1,0:T(2,128)(2,1)} copy(bf16[10,320,2,128]{1,3,2,0:T(8,128)(2,1)S(1)} %get-tuple-element.5) | data formatting | bytes 3276800
  167.1 6.8 %pad_maximum_fusion = bf16[10,64,2,5,2,128]{5,4,3,1,0,2:T(2,128)(2,1)S(1)} fusion(bf16[10,64,1,5,2,128]{5,4,3,1,0,2:T(2,128)(2,1)} %bitcast.29, bf16[10,64,1,5,2,128]{5,4,3,1,0,2:T(2,128)(2,1)} %bitcast.28), kind=kLoop, calls=%fused_computation.15 | loop fusion | flops 1638400 | bytes 6553600 | tf_op jit(solution)/shard_map/stack | solution.py:45
  174.0 2.2 copy.19
  176.2 153.7 %all_to_all.33 = bf16[10,64,2,5,2,128]{5,4,3,0,2,1:T(2,128)(2,1)S(1)} all-to-all(bf16[10,64,2,5,2,128]{5,4,3,0,2,1:T(2,128)(2,1)S(1)} %copy.19), channel_id=1, replica_groups=mesh['lat'=64,'mem'=8] {'lat'}, dimensions={1} | all-to-all | bytes 6553600 | tf_op jit(solution)/shard_map/all_to_all | solution.py:46
  329.9 2.2 copy.20
  332.1 2.2 fusion.13
  334.4 71.6 %all-reduce.2.cloned.1.call-done = f32[2,5,128,128]{3,2,1,0:T(8,128)} async-done(((f32[2,5,128,128]{3,2,1,0:T(8,128)}), f32[2,5,128,128]{3,2,1,0:T(8,128)}) %all-reduce.2.cloned.1.call-update) | async-done | bytes 655376 | tf_op jit(solution)/shard_map/psum | solution.py:51
  406.0 1.5 dynamic-slice_multiply_fusion
  (8 shorter events, 0.2 us)
Async XLA Ops:
  6.5 94.0 %copy-start = (bf16[1,1,128,2688]{3,2,1,0:T(8,128)(2,1)S(1)}, bf16[1,1,128,2688]{3,2,1,0:T(8,128)(2,1)}, u32[]{:S(2)}) copy-start(bf16[1,1,128,2688]{3,2,1,0:T(8,128)(2,1)} %param.4) | copy-start | bytes 2064388
  102.6 46.0 %copy-start.1 = (bf16[10,64,640]{2,1,0:T(8,128)(2,1)S(1)}, bf16[10,64,640]{2,1,0:T(8,128)(2,1)}, u32[]{:S(2)}) copy-start(bf16[10,64,640]{2,1,0:T(8,128)(2,1)} %param.7) | copy-start | bytes 2457604
  105.0 41.2 %all-to-all-start = ((bf16[64,2,1280]{2,1,0:T(2,128)(2,1)}), bf16[64,2,1280]{2,1,0:T(2,128)(2,1)S(1)}, u32[]{:S(2)}, u32[]{:S(2)}) async-start(bf16[64,2,1280]{2,1,0:T(2,128)(2,1)} %reshape.166), calls=%async_computation | async-start | bytes 655360 | tf_op jit(solution)/shard_map/all_to_all | solution.py:38
  124.1 281.9 %all-reduce.2.cloned.1.call-start = ((), (), s32[]{:S(2)}) async-start(), calls=%async_computation.2 | async-start | bytes 1310720 | tf_op jit(solution)/shard_map/psum | solution.py:51
Sparse Core Ops, SparseCore 0:
  334.5 71.4 all-reduce.1
where the time goes:
time: 416 us; the launch traced here: 414 us
  blocking collectives  154 us (37%)
  other arithmetic  105 us (25%)
  waiting for transfers between devices  92.8 us (22%)
  local copies, waits for them, and re-layouts  24.7 us (6%)
  starting transfers between devices  19.2 us (5%)
  between operations  14.2 us (3%)
  matrix products  5.32 us (1%)
    all_to_all x1, blocking collectives, per_device(): lax.all_to_all(folded, 'lat', split_axis=1, concat_axis=0, tiled=True)  154 us
    another operation x1, other arithmetic  93.3 us
    psum x1, waiting for transfers between devices, per_device(): whole = lax.psum(terms, 'mem')  71.6 us
    all_to_all x1, waiting for transfers between devices, per_device(): lax.all_to_all(fourier, 'lat', split_axis=0, concat_axis=1, tiled=True)  21.2 us
    all_to_all x1, starting transfers between devices, per_device(): lax.all_to_all(fourier, 'lat', split_axis=0, concat_axis=1, tiled=True)  19.1 us
    unnamed x9, local copies, waits for them, and re-layouts  12.3 us
  transfers between devices with their start and end apart: 2, of which 2 were waited for; matrix products, arithmetic and copies ran while one was open for 0% of the time, Pallas kernels for 0%

commit v1 on v0

v1 whole, which is shorter than its diff:
```python
import jax
import jax.numpy as jnp
from jax import lax
from jax.experimental import pallas as pl
from jax.experimental.pallas import tpu as pltpu
from jax.sharding import PartitionSpec as P

MESH = pl.DeviceIdType.MESH
F32 = jnp.float32
BF16 = jnp.bfloat16
Z, X, D = 16, 4, 8
GROUP = X * D
LEV, LONS, M = 128, 2688, 640
PAIRS = 5
OWN = 10
COS = (1.0, -19.739208221435547, 64.93939208984375, -85.45681762695312, 60.24457931518555,
       -26.425565719604492, 7.898900985717773, -1.6961979866027832, 0.24304766952991486)
SIN = (6.2831854820251465, -41.34170150756836, 81.6052474975586, -76.70585632324219, 42.05867385864258,
       -15.094411849975586, 3.818404197692871, -0.7120527029037476, 0.09126123040914536)


def iota(shape, dim):
    return lax.broadcasted_iota(jnp.int32, shape, dim)


def dot(a, b, ca, cb):
    return lax.dot_general(a, b, (((ca,), (cb,)), ((), ())), preferred_element_type=F32)


def poly(coefficients, v):
    total = jnp.full_like(v, coefficients[-1])
    for value in coefficients[-2::-1]:
        total = total * v + value
    return total


def unit(product, count, inverse):
    turns = jnp.floor(product * inverse + 0.5)
    u = (product - turns * count) * inverse
    v = u * u
    return poly(COS, v), -u * poly(SIN, v)


def one_hot(condition):
    return jnp.where(condition, 1.0, 0.0).astype(BF16)


def total_wave(dest, k):
    t = (dest & 7) + 8 * k
    zz = (t * 205) >> 10
    return 20 * zz + 5 * (dest >> 3) + (t - 5 * zz)


def kernel(count_ref, wave_ref, waves_ref, field_ref, leg_ref, out_ref,
           fm, tbl, base, zs, zr, xs, xr, p256, prow, pcol, lr, lu, lv, lul, lvl, lw,
           psa, psb, psc, pra, prb, prc, ab, mt, acc, rs, rr, mm,
           zs_sem, zr_sem, xs_sem, xr_sem, ps_sem, pr_sem, rs_sem, rr_sem, ms_sem, mr_sem):
    lat = lax.axis_index("lat")
    d = lax.axis_index("mem")
    z, x = lat // X, lat % X
    me = x * D + d

    def z_partner(o):
        other = (z + o) % Z
        return other, (other * X + x, d)

    def plane_partner(o):
        other = (me + o) % GROUP
        return other, (z * X + other // D, other % D)

    barrier = pltpu.get_barrier_semaphore()

    def greet_z(o, carry):
        pl.semaphore_signal(barrier, inc=1, device_id=z_partner(o)[1], device_id_type=MESH)
        return carry

    def greet_plane(o, carry):
        pl.semaphore_signal(barrier, inc=1, device_id=plane_partner(o)[1], device_id_type=MESH)
        return carry

    lax.fori_loop(1, Z, greet_z, 0)
    lax.fori_loop(1, GROUP, greet_plane, 0)

    count = count_ref[0].astype(F32)
    inverse = 1.0 / jnp.full((128, 128), count, F32)
    fm[...] = jnp.where(iota((LEV, LONS), 1) < count_ref[0], field_ref[...].astype(F32), 0.0).astype(BF16)
    wave_row = waves_ref[...].astype(F32)
    p_row = iota((128, M), 0)

    def make_base(j, carry):
        slot = 10 * (p_row >> 1) + 2 * j + (p_row & 1)
        wave = jnp.sum(jnp.where(iota((128, M), 1) == slot, wave_row, 0.0), axis=1, keepdims=True)
        wave = jnp.broadcast_to(wave, (128, 128))
        c, s = unit(wave * iota((128, 128), 1).astype(F32), count, inverse)
        base[j, 0] = c
        base[j, 1] = s
        c, s = unit(wave * 128.0, count, inverse)
        base[j, 2] = c
        base[j, 3] = s
        return carry

    lax.fori_loop(0, PAIRS, make_base, 0)
    pl.semaphore_wait(barrier, Z - 1 + GROUP - 1)

    def transform(j, carry):
        def rows(b, inner):
            at = pl.ds(pl.multiple_of(b * 32, 32), 32)
            c, s = base[j, 0, at, :], base[j, 1, at, :]
            cw, sw = base[j, 2, at, :], base[j, 3, at, :]
            for a in range(LONS // 128):
                tbl[0, at, a * 128:(a + 1) * 128] = c.astype(BF16)
                tbl[1, at, a * 128:(a + 1) * 128] = s.astype(BF16)
                c, s = c * cw - s * sw, c * sw + s * cw
            return inner

        lax.fori_loop(0, 4, rows, 0)
        summed = dot(tbl[...].reshape(256, LONS), fm[...], 1, 1) / count
        both = summed.reshape(2, Z, 8, LEV)
        zs[j] = jnp.concatenate([both[0], both[1]], axis=1).astype(BF16)
        zr[j, z] = zs[j, z]

        def send(o, inner):
            other, device = z_partner(o)
            pltpu.make_async_remote_copy(
                src_ref=zs.at[j, other], dst_ref=zr.at[j, z], send_sem=zs_sem, recv_sem=zr_sem.at[j],
                device_id=device, device_id_type=MESH).start()
            return inner

        lax.fori_loop(1, Z, send, 0)
        return carry

    lax.fori_loop(0, PAIRS, transform, 0)

    o_row, o_col = iota((256, 256), 0), iota((256, 256), 1)
    p256[...] = one_hot(o_col == (o_row & 15) * 16 + (o_row >> 4))
    o_row, o_col = iota((128, 128), 0), iota((128, 128), 1)
    prow[...] = one_hot(o_col == ((o_row >> 4) & 1) * 64 + 4 * (o_row & 15) + (o_row >> 5))
    c_row = iota((256, 1), 0)
    i_main = total_wave(c_row >> 3, c_row & 7)
    i_left = total_wave(c_row >> 3, 8 + (c_row & 1))
    n_col = iota((256, M), 1)
    pcol[0:256] = one_hot(n_col == M - 1 - i_main)
    pcol[256:512] = one_hot(n_col == i_main)
    pcol[512:768] = one_hot(n_col == M - 1 - i_left)
    pcol[768:1024] = one_hot(n_col == i_left)

    lane_slot = (iota((1, 128), 1) >> 4) & 1
    left_j = (c_row >> 1) & 3

    def legendre(j, carry):
        lr[j] = dot(prow[...], leg_ref[pl.ds(2 * j, 2)].reshape(128, M), 1, 0).astype(BF16)
        w0 = wave_ref[10 * lat + 2 * j]
        w1 = wave_ref[10 * lat + 2 * j + 1]
        low = jnp.minimum(w0, w1)
        small = jnp.where(lane_slot == 0, w0, w1) == low
        put = pcol[...]
        moved = dot(put, lr[j], 1, 1)
        upper, lower, upper_left, lower_left = (moved[a * 256:(a + 1) * 256] for a in range(4))
        lu[j] = jnp.where(small, upper, 0.0).astype(BF16)
        lv[j] = jnp.where(small, jnp.where(i_main >= low, lower, 0.0),
                          jnp.where(i_main < low, upper, 0.0)).astype(BF16)
        here = left_j == lax.rem(j, 4)
        lul[j] = jnp.where(here & small, upper_left, 0.0).astype(BF16)
        lvl[j] = jnp.where(small, jnp.where(here & (i_left >= low), lower_left, 0.0),
                           jnp.where(here & (i_left < low), upper_left, 0.0)).astype(BF16)
        pick = one_hot((iota((16, M), 0) == 2 + j) & (iota((16, M), 1) == M - 1 - low))
        lw[j] = jnp.where(small, 0.0, dot(pick, lr[j], 1, 1)).astype(BF16)
        for xx in range(X):
            wave = wave_ref[10 * (X * z + xx) + 2 * j]
            mt[j, xx * 8:(xx + 1) * 8, :] = jnp.full((8, 128), jnp.minimum(wave, M - 1 - wave), jnp.int32)
        return carry

    lax.fori_loop(0, PAIRS, legendre, 0)

    def swap_rows(j):
        pltpu.make_async_copy(zr.at[j, 0:Z - 1], zr.at[j, 0:Z - 1], zr_sem.at[j]).wait()
        moved = dot(p256[...], zr[j].reshape(256, LEV), 1, 0).astype(BF16)
        for q in range(2):
            for xx in range(X):
                at = (q * 8 + xx * 2) * 16
                xs[j, xx, :, q * 128:(q + 1) * 128] = moved[at:at + 32]
        xr[j, x] = xs[j, x]

        def send(o, carry):
            other = (x + o) % X
            pltpu.make_async_remote_copy(
                src_ref=xs.at[j, other], dst_ref=xr.at[j, x], send_sem=xs_sem, recv_sem=xr_sem.at[j],
                device_id=(z * X + other, d), device_id_type=MESH).start()
            return carry

        lax.fori_loop(1, X, send, 0)

    def rows_in(j):
        pltpu.make_async_copy(xr.at[j, 0:X - 1], xr.at[j, 0:X - 1], xr_sem.at[j]).wait()

    def both_kinds(up, low):
        return jnp.concatenate([up.reshape(GROUP, 8, 256), low.reshape(GROUP, 8, 256)], axis=1).astype(BF16)

    def spectral(j, target, place):
        rhs = xr[j].reshape(128, 256)
        target[:, place:place + 16, :] = both_kinds(dot(lu[j], rhs, 1, 0), dot(lv[j], rhs, 1, 0))

    def send_plane(stage, source, target):
        target[me] = source[me]

        def send(o, carry):
            other, device = plane_partner(o)
            pltpu.make_async_remote_copy(
                src_ref=source.at[other], dst_ref=target.at[me], send_sem=ps_sem.at[stage],
                recv_sem=pr_sem.at[stage], device_id=device, device_id_type=MESH).start()
            return carry

        lax.fori_loop(1, GROUP, send, 0)

    swap_rows(0)
    swap_rows(1)
    rows_in(0)
    spectral(0, psa, 0)
    rows_in(1)
    spectral(1, psa, 16)
    send_plane(0, psa, pra)
    swap_rows(2)
    swap_rows(3)
    rows_in(2)
    spectral(2, psb, 0)
    rows_in(3)
    spectral(3, psb, 16)
    up, low = jnp.zeros((256, 256), F32), jnp.zeros((256, 256), F32)
    for j in range(4):
        rhs = xr[j].reshape(128, 256)
        up += dot(lul[j], rhs, 1, 0)
        low += dot(lvl[j], rhs, 1, 0)
    psb[:, 32:48, :] = both_kinds(up, low)
    send_plane(1, psb, prb)
    swap_rows(4)
    rows_in(4)
    spectral(4, psc, 0)
    rhs = xr[4].reshape(128, 256)
    extra = jnp.zeros((16, 256), F32)
    for j in range(PAIRS):
        extra += dot(lw[j], xr[j].reshape(128, 256), 1, 0)
    up = dot(lul[4], rhs, 1, 0).reshape(GROUP, 8, 256) + extra[0:8][None]
    psc[:, 16:32, :] = both_kinds(up, dot(lvl[4], rhs, 1, 0))
    send_plane(2, psc, prc)

    def arrived(stage, target, subs):
        pltpu.make_async_copy(target.at[0:GROUP - 1], target.at[0:GROUP - 1], pr_sem.at[stage]).wait()
        for b, sub in enumerate(subs):
            for g in range(2):
                piece = target[g * 16:(g + 1) * 16, b * 16:(b + 1) * 16, :].reshape(256, 256)
                moved = dot(p256[...], piece, 1, 0).astype(BF16)
                ab[sub, :, g * 16:(g + 1) * 16, :] = moved.reshape(16, 16, 256)

    def halves(rows):
        return jnp.concatenate([rows[:, 0:128], rows[:, 128:256]], axis=0)

    def waves_of(js):
        tile = jnp.concatenate([mt[j] for j in js], axis=0)
        return jnp.concatenate([tile, tile], axis=0)

    def gram(k, ups, lows, js, first, extras=None):
        i = total_wave(me, k)
        up = halves(jnp.concatenate(ups, axis=0))
        low = halves(jnp.concatenate(lows, axis=0))
        waves = waves_of(js)
        inside = low * one_hot(waves <= i)
        outside = low * one_hot(waves > i)
        near = dot(low, inside, 0, 0)
        far = dot(up, up, 0, 0) + dot(low, outside, 0, 0)
        if extras is not None:
            far += dot(extras, extras * one_hot(waves_of(range(PAIRS)) == i), 0, 0)
        if first:
            acc[k, 0] = near
            acc[k, 1] = far
        else:
            acc[k, 0] += near
            acc[k, 1] += far

    arrived(0, pra, (0, 1))

    def gram_a(k, carry):
        gram(k, [ab[0, k], ab[1, k]], [ab[0, 8 + k], ab[1, 8 + k]], (0, 1), True)
        return carry

    lax.fori_loop(0, 8, gram_a, 0)
    arrived(1, prb, (2, 3, 5))

    def gram_b(k, carry):
        gram(k, [ab[2, k], ab[3, k]], [ab[2, 8 + k], ab[3, 8 + k]], (2, 3), False)
        return carry

    lax.fori_loop(0, 8, gram_b, 0)
    for kk in range(2):
        gram(8 + kk, [ab[5, 2 * j + kk] for j in range(4)], [ab[5, 8 + 2 * j + kk] for j in range(4)],
             (0, 1, 2, 3), True)
    arrived(2, prc, (4, 6))
    extras = halves(jnp.concatenate([ab[6, 2 + j] for j in range(PAIRS)], axis=0))

    lane = iota((16, 128), 1)

    def pack_send(k):
        for h in range(2):
            whole = acc[k, h]
            blocks = [whole[0:16]]
            for r in range(1, 4):
                folded = pltpu.roll(whole[16 * (8 - r):16 * (9 - r)], 16 * r, 1)
                blocks.append(jnp.where(lane >= 16 * r, whole[16 * r:16 * (r + 1)], folded))
            blocks.append(whole[64:80])
            rs[k, h * 80:(h + 1) * 80, :] = jnp.concatenate(blocks, axis=0).astype(BF16)
        owner = (d + 8 * k) // 5

        @pl.when(owner == z)
        def _():
            rr[z] = rs[k]

        @pl.when(owner != z)
        def _():
            pltpu.make_async_remote_copy(
                src_ref=rs.at[k], dst_ref=rr.at[z], send_sem=rs_sem, recv_sem=rr_sem,
                device_id=(owner * X + x, d), device_id_type=MESH).start()

    def gram_c(k, carry):
        gram(k, [ab[4, k]], [ab[4, 8 + k]], (4,), False, extras)
        pack_send(k)
        return carry

    lax.fori_loop(0, 8, gram_c, 0)

    def gram_d(kk, carry):
        gram(8 + kk, [ab[6, kk]], [ab[6, 8 + kk]], (4,), False, extras)
        pack_send(8 + kk)
        return carry

    lax.fori_loop(0, 2, gram_d, 0)

    u = (d + 3 * z) % 8
    holds = u < 5

    @pl.when(holds)
    def _():
        pltpu.make_async_copy(rr.at[0:Z - 1], rr.at[0:Z - 1], rr_sem).wait()
        total = rr[0].astype(F32)
        for a in range(1, Z):
            total += rr[a].astype(F32)
        total = total * 0.125
        for h in range(2):
            part = total[h * 80:(h + 1) * 80]
            blocks = [part[16 * r:16 * (r + 1)] for r in range(5)]
            for r in range(3, 0, -1):
                blocks.append(pltpu.roll(part[16 * r:16 * (r + 1)], 128 - 16 * r, 1))
            upper = jnp.concatenate(blocks, axis=0)
            keep = (iota((128, 128), 1) >> 4) >= (iota((128, 128), 0) >> 4)
            full = jnp.where(keep, upper, upper.T)
            mm[:, h] = full.reshape(8, 16, 128)
        out_ref[:, u] = mm[d]

        def send(o, carry):
            other = (d + o) % D
            pltpu.make_async_remote_copy(
                src_ref=mm.at[other], dst_ref=out_ref.at[:, u], send_sem=ms_sem, recv_sem=mr_sem,
                device_id=(lat, other), device_id_type=MESH).start()
            return carry

        lax.fori_loop(1, D, send, 0)

    @pl.when(holds)
    def _():
        pltpu.make_async_copy(out_ref.at[:, 0:4], out_ref.at[:, 0:4], mr_sem).wait()
        pltpu.make_async_copy(mm.at[0:7], mm.at[0:7], ms_sem).wait()

    @pl.when(jnp.logical_not(holds))
    def _():
        pltpu.make_async_copy(out_ref, out_ref, mr_sem).wait()

    for j in range(PAIRS):
        pltpu.make_async_copy(zs.at[j, 0:Z - 1], zs.at[j, 0:Z - 1], zs_sem).wait()
        pltpu.make_async_copy(xs.at[j, 0:X - 1], xs.at[j, 0:X - 1], xs_sem).wait()
    for stage, source in enumerate((psa, psb, psc)):
        pltpu.make_async_copy(source.at[0:GROUP - 1], source.at[0:GROUP - 1], ps_sem.at[stage]).wait()

    @pl.when(holds)
    def _():
        pltpu.make_async_copy(rs.at[0:OWN - 1], rs.at[0:OWN - 1], rs_sem).wait()

    @pl.when(jnp.logical_not(holds))
    def _():
        pltpu.make_async_copy(rs, rs, rs_sem).wait()


def per_device(field, lon_count, wave_order, legendre):
    vmem = pl.BlockSpec(memory_space=pltpu.VMEM)
    smem = pl.BlockSpec(memory_space=pltpu.SMEM)
    V = pltpu.VMEM
    scratch = [
        V((LEV, LONS), BF16), V((2, 128, LONS), BF16), V((PAIRS, 4, 128, 128), F32),
        V((PAIRS, Z, 16, LEV), BF16), V((PAIRS, Z, 16, LEV), BF16),
        V((PAIRS, X, 32, 256), BF16), V((PAIRS, X, 32, 256), BF16),
        V((256, 256), BF16), V((128, 128), BF16), V((1024, M), BF16), V((PAIRS, 128, M), BF16),
        V((PAIRS, 256, 128), BF16), V((PAIRS, 256, 128), BF16),
        V((PAIRS, 256, 128), BF16), V((PAIRS, 256, 128), BF16), V((PAIRS, 16, 128), BF16),
        V((GROUP, 32, 256), BF16), V((GROUP, 48, 256), BF16), V((GROUP, 32, 256), BF16),
        V((GROUP, 32, 256), BF16), V((GROUP, 48, 256), BF16), V((GROUP, 32, 256), BF16),
        V((7, 16, GROUP, 256), BF16), V((PAIRS, 32, 128), jnp.int32), V((OWN, 2, 128, 128), F32),
        V((OWN, 160, 128), BF16), V((Z, 160, 128), BF16), V((D, 2, 16, 128), F32),
        pltpu.SemaphoreType.DMA, pltpu.SemaphoreType.DMA((PAIRS,)),
        pltpu.SemaphoreType.DMA, pltpu.SemaphoreType.DMA((PAIRS,)),
        pltpu.SemaphoreType.DMA((3,)), pltpu.SemaphoreType.DMA((3,)),
        pltpu.SemaphoreType.DMA, pltpu.SemaphoreType.DMA,
        pltpu.SemaphoreType.DMA, pltpu.SemaphoreType.DMA,
    ]
    return pl.pallas_call(
        kernel,
        out_shape=jax.ShapeDtypeStruct((2, 5, 16, 128), F32),
        in_specs=[smem, smem, vmem, vmem, vmem],
        out_specs=vmem,
        scratch_shapes=scratch,
        compiler_params=pltpu.CompilerParams(
            collective_id=0, has_side_effects=True, vmem_limit_bytes=48 * 1024 * 1024),
    )(lon_count, wave_order, wave_order.reshape(1, M), field.reshape(LEV, LONS), legendre)


def solution(mesh):
    return jax.shard_map(
        per_device,
        mesh=mesh,
        in_specs=(P("mem", "lat", None, None), P("lat"), P(), P("lat", None, None)),
        out_specs=P(None, "lat", "mem", None),
        check_vma=False,
    )
```

time: 416 us -> 91.8 us (0.22)
  blocking collectives: 154 us -> 0 us
  other arithmetic: 105 us -> 0 us
  waiting for transfers between devices: 92.8 us -> 0 us
  Pallas kernels: 0 us -> 87.3 us
  local copies, waits for them, and re-layouts: 24.7 us -> 3.64 us
  starting transfers between devices: 19.2 us -> 0 us
  between operations: 14.2 us -> 0.67 us
  matrix products: 5.32 us -> 0 us
    all_to_all x1 -> x0, blocking collectives: 154 us -> none  [per_device(): lax.all_to_all(folded, 'lat', split_axis=1, concat_axis=0, tiled=True)]
    another operation x3 -> x0, other arithmetic: 101 us -> none
    pallas_call x0 -> x1, Pallas kernels: none -> 87.3 us  [per_device(): pl.pallas_call(kernel, out_shape=jax.ShapeDtypeStruct((2, 5, 16, 128), F3...]
    psum x1 -> x0, waiting for transfers between devices: 71.6 us -> none  [per_device(): whole = lax.psum(terms, 'mem')]
    all_to_all x1 -> x0, waiting for transfers between devices: 21.2 us -> none  [per_device(): lax.all_to_all(fourier, 'lat', split_axis=0, concat_axis=1, tiled=True)]
    all_to_all x1 -> x0, starting transfers between devices: 19.1 us -> none  [per_device(): lax.all_to_all(fourier, 'lat', split_axis=0, concat_axis=1, tiled=True)]
    unnamed x9 -> x7, local copies, waits for them, and re-layouts: 12.3 us -> 2.89 us
    dot_general x3 -> x0, matrix products: 5.32 us -> none  [the longest x1 2.22 us: per_device(): jnp.einsum('sxhica,sxhicb->hiab', received, received, preferred_element_t...]
  transfers between devices with their start and end apart: 2 -> 0, of which waited for: 2 -> 0; matrix products, arithmetic and copies ran while one was open for 0% -> 0% of each run, Pallas kernels for 0% -> 0%
where the time goes in v1:
time: 91.8 us; the launch traced here: 91.6 us
  Pallas kernels  87.3 us (95%)
  local copies, waits for them, and re-layouts  3.64 us (4%)
    pallas_call x1, Pallas kernels, per_device(): pl.pallas_call(kernel, out_shape=jax.ShapeDtypeStruct((2, 5, 16, 128), F3...  87.3 us
    unnamed x7, local copies, waits for them, and re-layouts  2.89 us

profile of v1, /device:TPU:1, one launch (start us, length us, event | category | flops | bytes accessed | tf_op | source)
XLA Modules:
  0.0 91.6 jit_solution(15814571906729171128)
XLA Ops:
  0.7 0.0 copy-start.2
  0.7 0.8 reshape.6.waves_ref
  1.4 0.0 copy-done.2
  1.4 0.0 copy-start
  1.4 1.1 %copy-done = bf16[10,64,640]{2,1,0:T(8,128)(2,1)S(1)} copy-done((bf16[10,64,640]{2,1,0:T(8,128)(2,1)S(1)}, bf16[10,64,640]{2,1,0:T(8,128)(2,1)}, u32[]{:S(2)}) %copy-start) | copy-done | bytes 819224
  2.6 0.0 copy-start.1
  2.6 1.1 %copy-done.1 = bf16[1,1,128,2688]{3,2,1,0:T(8,128)(2,1)S(1)} copy-done((bf16[1,1,128,2688]{3,2,1,0:T(8,128)(2,1)S(1)}, bf16[1,1,128,2688]{3,2,1,0:T(8,128)(2,1)}, u32[]{:S(2)}) %copy-start.1) | copy-done | bytes 688152
  3.7 87.3 %shard_map.46 = f32[2,5,16,128]{3,2,1,0:T(8,128)S(1)} custom-call(s32[1]{0:T(128)S(6)} %copy.6.count_ref, s32[640]{0:T(1024)S(1)} %copy-done.2, s32[1,640]{1,0:T(1,128)S(1)} %reshape.6.waves_ref, bf16[128,2688]{1,0:T(8,128)(2,1)S(1)} %bitcast.1, bf16[10,64,640]{2,1,0:T(8,128)(2,1)S(1)} %copy-done), custom_call_target="tpu_custom_call" | custom-call | tf_op jit(solution)/shard_map/pallas_call | solution.py:411
  90.9 0.6 copy.7
Async XLA Ops:
  0.7 0.8 copy-start.2
  1.4 1.1 %copy-start = (bf16[10,64,640]{2,1,0:T(8,128)(2,1)S(1)}, bf16[10,64,640]{2,1,0:T(8,128)(2,1)}, u32[]{:S(2)}) copy-start(bf16[10,64,640]{2,1,0:T(8,128)(2,1)} %leg_ref.1) | copy-start | bytes 2457604
  2.6 1.1 %copy-start.1 = (bf16[1,1,128,2688]{3,2,1,0:T(8,128)(2,1)S(1)}, bf16[1,1,128,2688]{3,2,1,0:T(8,128)(2,1)}, u32[]{:S(2)}) copy-start(bf16[1,1,128,2688]{3,2,1,0:T(8,128)(2,1)} %param.4) | copy-start | bytes 2064388

commit v2 on v1

--- a/solution.py
+++ b/solution.py
@@ -10,8 +10,9 @@
 BF16 = jnp.bfloat16
 Z, X, D = 16, 4, 8
 GROUP = X * D
-LEV, LONS, M = 128, 2688, 640
+LEV, LONS, M, NLAT = 128, 2688, 640, 64
 PAIRS = 5
+EXTRA = (6, 7, 14, 4, 5)
 OWN = 10
 COS = (1.0, -19.739208221435547, 64.93939208984375, -85.45681762695312, 60.24457931518555,
        -26.425565719604492, 7.898900985717773, -1.6961979866027832, 0.24304766952991486)
@@ -52,20 +53,25 @@
 
 
 def kernel(count_ref, wave_ref, waves_ref, field_ref, leg_ref, out_ref,
-           fm, tbl, base, zs, zr, xs, xr, p256, prow, pcol, lr, lu, lv, lul, lvl, lw,
-           psa, psb, psc, pra, prb, prc, ab, mt, acc, rs, rr, mm,
-           zs_sem, zr_sem, xs_sem, xr_sem, ps_sem, pr_sem, rs_sem, rr_sem, ms_sem, mr_sem):
+           fi, li, fm, tbl, base, zsa, zsb, zsc, zra, zrb, zrc, xs, xr, p256, prow, pcol, lr, lu, lv, lul, lvl, lw,
+           psa, psb, psc, pra, prb, prc, ab, mt, acc, rs, r1, r2s, r2, mm,
+           in_sem, zs_sem, zr_sem, xs_sem, xr_sem, ps_sem, pr_sem, r1s_sem, r1_sem, r2s_sem, r2_sem, ms_sem, mr_sem):
+    field_in = pltpu.make_async_copy(field_ref, fi, in_sem.at[0])
+    leg_in = pltpu.make_async_copy(leg_ref, li, in_sem.at[1])
+    field_in.start()
+    leg_in.start()
     lat = lax.axis_index("lat")
     d = lax.axis_index("mem")
     z, x = lat // X, lat % X
     me = x * D + d
 
     def z_partner(o):
-        other = (z + o) % Z
+        far = 8 - (o + 1) // 2
+        other = (z + far + (1 - o % 2) * (Z - 2 * far)) % Z
         return other, (other * X + x, d)
 
     def plane_partner(o):
-        other = (me + o) % GROUP
+        other = (me + 11 * o) % GROUP
         return other, (z * X + other // D, other % D)
 
     barrier = pltpu.get_barrier_semaphore()
@@ -78,13 +84,12 @@
         pl.semaphore_signal(barrier, inc=1, device_id=plane_partner(o)[1], device_id_type=MESH)
         return carry
 
-    lax.fori_loop(1, Z, greet_z, 0)
+    lax.fori_loop(0, Z - 1, greet_z, 0)
     lax.fori_loop(1, GROUP, greet_plane, 0)
 
     count = count_ref[0].astype(F32)
     inverse = 1.0 / jnp.full((128, 128), count, F32)
-    fm[...] = jnp.where(iota((LEV, LONS), 1) < count_ref[0], field_ref[...].astype(F32), 0.0).astype(BF16)
-    wave_row = waves_ref[...].astype(F32)
+    wave_row = waves_ref[...].astype(F32).reshape(1, M)
     p_row = iota((128, M), 0)
 
     def make_base(j, carry):
@@ -100,9 +105,10 @@
         return carry
 
     lax.fori_loop(0, PAIRS, make_base, 0)
-    pl.semaphore_wait(barrier, Z - 1 + GROUP - 1)
-
-    def transform(j, carry):
+    field_in.wait()
+    fm[...] = jnp.where(iota((LEV, LONS), 1) < count_ref[0], fi[...].astype(F32), 0.0).astype(BF16)
+
+    def transform(j, target, place):
         def rows(b, inner):
             at = pl.ds(pl.multiple_of(b * 32, 32), 32)
             c, s = base[j, 0, at, :], base[j, 1, at, :]
@@ -116,20 +122,29 @@
         lax.fori_loop(0, 4, rows, 0)
         summed = dot(tbl[...].reshape(256, LONS), fm[...], 1, 1) / count
         both = summed.reshape(2, Z, 8, LEV)
-        zs[j] = jnp.concatenate([both[0], both[1]], axis=1).astype(BF16)
-        zr[j, z] = zs[j, z]
-
-        def send(o, inner):
+        target[:, place * 16:place * 16 + 16, :] = jnp.concatenate([both[0], both[1]], axis=1).astype(BF16)
+
+    def send_z(stage, source, target):
+        target[z] = source[z]
+
+        def send(o, carry):
             other, device = z_partner(o)
             pltpu.make_async_remote_copy(
-                src_ref=zs.at[j, other], dst_ref=zr.at[j, z], send_sem=zs_sem, recv_sem=zr_sem.at[j],
-                device_id=device, device_id_type=MESH).start()
-            return inner
-
-        lax.fori_loop(1, Z, send, 0)
-        return carry
-
-    lax.fori_loop(0, PAIRS, transform, 0)
+                src_ref=source.at[other], dst_ref=target.at[z], send_sem=zs_sem.at[stage],
+                recv_sem=zr_sem.at[stage], device_id=device, device_id_type=MESH).start()
+            return carry
+
+        lax.fori_loop(0, Z - 1, send, 0)
+
+    transform(0, zsa, 0)
+    pl.semaphore_wait(barrier, Z - 1 + GROUP - 1)
+    send_z(0, zsa, zra)
+    transform(1, zsb, 0)
+    transform(2, zsb, 1)
+    send_z(1, zsb, zrb)
+    transform(3, zsc, 0)
+    transform(4, zsc, 1)
+    send_z(2, zsc, zrc)
 
     o_row, o_col = iota((256, 256), 0), iota((256, 256), 1)
     p256[...] = one_hot(o_col == (o_row & 15) * 16 + (o_row >> 4))
@@ -147,8 +162,8 @@
     lane_slot = (iota((1, 128), 1) >> 4) & 1
     left_j = (c_row >> 1) & 3
 
-    def legendre(j, carry):
-        lr[j] = dot(prow[...], leg_ref[pl.ds(2 * j, 2)].reshape(128, M), 1, 0).astype(BF16)
+    def legendre(j):
+        lr[j] = dot(prow[...], li[2 * j:2 * j + 2].reshape(128, M), 1, 0).astype(BF16)
         w0 = wave_ref[10 * lat + 2 * j]
         w1 = wave_ref[10 * lat + 2 * j + 1]
         low = jnp.minimum(w0, w1)
@@ -159,22 +174,22 @@
         lu[j] = jnp.where(small, upper, 0.0).astype(BF16)
         lv[j] = jnp.where(small, jnp.where(i_main >= low, lower, 0.0),
                           jnp.where(i_main < low, upper, 0.0)).astype(BF16)
-        here = left_j == lax.rem(j, 4)
+        here = left_j == j % 3
         lul[j] = jnp.where(here & small, upper_left, 0.0).astype(BF16)
         lvl[j] = jnp.where(small, jnp.where(here & (i_left >= low), lower_left, 0.0),
                            jnp.where(here & (i_left < low), upper_left, 0.0)).astype(BF16)
-        pick = one_hot((iota((16, M), 0) == 2 + j) & (iota((16, M), 1) == M - 1 - low))
+        pick = one_hot((iota((16, M), 0) == EXTRA[j]) & (iota((16, M), 1) == M - 1 - low))
         lw[j] = jnp.where(small, 0.0, dot(pick, lr[j], 1, 1)).astype(BF16)
         for xx in range(X):
             wave = wave_ref[10 * (X * z + xx) + 2 * j]
             mt[j, xx * 8:(xx + 1) * 8, :] = jnp.full((8, 128), jnp.minimum(wave, M - 1 - wave), jnp.int32)
-        return carry
-
-    lax.fori_loop(0, PAIRS, legendre, 0)
-
-    def swap_rows(j):
-        pltpu.make_async_copy(zr.at[j, 0:Z - 1], zr.at[j, 0:Z - 1], zr_sem.at[j]).wait()
-        moved = dot(p256[...], zr[j].reshape(256, LEV), 1, 0).astype(BF16)
+
+    def rows_along_z(stage, source):
+        pltpu.make_async_copy(source.at[0:Z - 1], source.at[0:Z - 1], zr_sem.at[stage]).wait()
+
+    def swap_rows(j, source, place):
+        piece = source[:, place * 16:place * 16 + 16, :].reshape(256, LEV)
+        moved = dot(p256[...], piece, 1, 0).astype(BF16)
         for q in range(2):
             for xx in range(X):
                 at = (q * 8 + xx * 2) * 16
@@ -212,35 +227,46 @@
 
         lax.fori_loop(1, GROUP, send, 0)
 
-    swap_rows(0)
-    swap_rows(1)
+    def left_over(js, target, place):
+        up, low = jnp.zeros((256, 256), F32), jnp.zeros((256, 256), F32)
+        extra = jnp.zeros((16, 256), F32)
+        for j in js:
+            rhs = xr[j].reshape(128, 256)
+            up += dot(lul[j], rhs, 1, 0)
+            low += dot(lvl[j], rhs, 1, 0)
+            extra += dot(lw[j], rhs, 1, 0)
+        up = up.reshape(GROUP, 8, 256) + extra[0:8][None]
+        low = low.reshape(GROUP, 8, 256) + extra[8:16][None]
+        target[:, place:place + 16, :] = both_kinds(up, low)
+
+    leg_in.wait()
+    legendre(0)
+    rows_along_z(0, zra)
+    swap_rows(0, zra, 0)
+    legendre(1)
     rows_in(0)
     spectral(0, psa, 0)
+    send_plane(0, psa, pra)
+    legendre(2)
+    rows_along_z(1, zrb)
+    swap_rows(1, zrb, 0)
+    swap_rows(2, zrb, 1)
+    legendre(3)
     rows_in(1)
-    spectral(1, psa, 16)
-    send_plane(0, psa, pra)
-    swap_rows(2)
-    swap_rows(3)
+    spectral(1, psb, 0)
     rows_in(2)
-    spectral(2, psb, 0)
+    spectral(2, psb, 16)
+    left_over((0, 1, 2), psb, 32)
+    send_plane(1, psb, prb)
+    legendre(4)
+    rows_along_z(2, zrc)
+    swap_rows(3, zrc, 0)
+    swap_rows(4, zrc, 1)
     rows_in(3)
-    spectral(3, psb, 16)
-    up, low = jnp.zeros((256, 256), F32), jnp.zeros((256, 256), F32)
-    for j in range(4):
-        rhs = xr[j].reshape(128, 256)
-        up += dot(lul[j], rhs, 1, 0)
-        low += dot(lvl[j], rhs, 1, 0)
-    psb[:, 32:48, :] = both_kinds(up, low)
-    send_plane(1, psb, prb)
-    swap_rows(4)
+    spectral(3, psc, 0)
     rows_in(4)
-    spectral(4, psc, 0)
-    rhs = xr[4].reshape(128, 256)
-    extra = jnp.zeros((16, 256), F32)
-    for j in range(PAIRS):
-        extra += dot(lw[j], xr[j].reshape(128, 256), 1, 0)
-    up = dot(lul[4], rhs, 1, 0).reshape(GROUP, 8, 256) + extra[0:8][None]
-    psc[:, 16:32, :] = both_kinds(up, dot(lvl[4], rhs, 1, 0))
+    spectral(4, psc, 16)
+    left_over((3, 4), psc, 32)
     send_plane(2, psc, prc)
 
     def arrived(stage, target, subs):
@@ -258,7 +284,7 @@
         tile = jnp.concatenate([mt[j] for j in js], axis=0)
         return jnp.concatenate([tile, tile], axis=0)
 
-    def gram(k, ups, lows, js, first, extras=None):
+    def gram(k, ups, lows, js, first, extras=None, extra_js=()):
         i = total_wave(me, k)
         up = halves(jnp.concatenate(ups, axis=0))
         low = halves(jnp.concatenate(lows, axis=0))
@@ -268,7 +294,7 @@
         near = dot(low, inside, 0, 0)
         far = dot(up, up, 0, 0) + dot(low, outside, 0, 0)
         if extras is not None:
-            far += dot(extras, extras * one_hot(waves_of(range(PAIRS)) == i), 0, 0)
+            far += dot(extras, extras * one_hot(waves_of(extra_js) == i), 0, 0)
         if first:
             acc[k, 0] = near
             acc[k, 1] = far
@@ -276,27 +302,36 @@
             acc[k, 0] += near
             acc[k, 1] += far
 
-    arrived(0, pra, (0, 1))
+    arrived(0, pra, (0,))
 
     def gram_a(k, carry):
-        gram(k, [ab[0, k], ab[1, k]], [ab[0, 8 + k], ab[1, 8 + k]], (0, 1), True)
+        gram(k, [ab[0, k]], [ab[0, 8 + k]], (0,), True)
         return carry
 
     lax.fori_loop(0, 8, gram_a, 0)
-    arrived(1, prb, (2, 3, 5))
+    arrived(1, prb, (1, 2, 5))
+    extras_b = halves(jnp.concatenate([ab[5, EXTRA[j]] for j in (0, 1, 2)], axis=0))
 
     def gram_b(k, carry):
-        gram(k, [ab[2, k], ab[3, k]], [ab[2, 8 + k], ab[3, 8 + k]], (2, 3), False)
+        gram(k, [ab[1, k], ab[2, k]], [ab[1, 8 + k], ab[2, 8 + k]], (1, 2), False, extras_b, (0, 1, 2))
         return carry
 
     lax.fori_loop(0, 8, gram_b, 0)
     for kk in range(2):
-        gram(8 + kk, [ab[5, 2 * j + kk] for j in range(4)], [ab[5, 8 + 2 * j + kk] for j in range(4)],
-             (0, 1, 2, 3), True)
-    arrived(2, prc, (4, 6))
-    extras = halves(jnp.concatenate([ab[6, 2 + j] for j in range(PAIRS)], axis=0))
+        gram(8 + kk, [ab[5, 2 * j + kk] for j in range(3)], [ab[5, 8 + 2 * j + kk] for j in range(3)],
+             (0, 1, 2), True, extras_b, (0, 1, 2))
+    arrived(2, prc, (3, 4, 6))
+    extras_c = halves(jnp.concatenate([ab[6, EXTRA[j]] for j in (3, 4)], axis=0))
 
     lane = iota((16, 128), 1)
+
+    behind = 1 + d % 2
+
+    def owner_of(k):
+        return (d + 8 * k) // 5
+
+    def toward(k):
+        return (owner_of(k) - z + Z + behind) % 4 - behind
 
     def pack_send(k):
         for h in range(2):
@@ -307,41 +342,61 @@
                 blocks.append(jnp.where(lane >= 16 * r, whole[16 * r:16 * (r + 1)], folded))
             blocks.append(whole[64:80])
             rs[k, h * 80:(h + 1) * 80, :] = jnp.concatenate(blocks, axis=0).astype(BF16)
-        owner = (d + 8 * k) // 5
-
-        @pl.when(owner == z)
-        def _():
-            rr[z] = rs[k]
-
-        @pl.when(owner != z)
+        step = toward(k)
+        seat = step + behind
+
+        @pl.when(step != 0)
         def _():
             pltpu.make_async_remote_copy(
-                src_ref=rs.at[k], dst_ref=rr.at[z], send_sem=rs_sem, recv_sem=rr_sem,
-                device_id=(owner * X + x, d), device_id_type=MESH).start()
+                src_ref=rs.at[k], dst_ref=r1.at[k, seat - (seat + 3 - behind) // 4], send_sem=r1s_sem,
+                recv_sem=r1_sem.at[k], device_id=(((z + step + Z) % Z) * X + x, d), device_id_type=MESH).start()
 
     def gram_c(k, carry):
-        gram(k, [ab[4, k]], [ab[4, 8 + k]], (4,), False, extras)
+        gram(k, [ab[3, k], ab[4, k]], [ab[3, 8 + k], ab[4, 8 + k]], (3, 4), False, extras_c, (3, 4))
         pack_send(k)
         return carry
 
+    def gram_d(kk, carry):
+        gram(8 + kk, [ab[6, kk], ab[6, 2 + kk]], [ab[6, 8 + kk], ab[6, 10 + kk]], (3, 4), False, extras_c, (3, 4))
+        pack_send(8 + kk)
+        return carry
+
     lax.fori_loop(0, 8, gram_c, 0)
-
-    def gram_d(kk, carry):
-        gram(8 + kk, [ab[6, kk]], [ab[6, 8 + kk]], (4,), False, extras)
-        pack_send(8 + kk)
-        return carry
-
     lax.fori_loop(0, 2, gram_d, 0)
+
+    def level_two(k, carry):
+        @pl.when(toward(k) == 0)
+        def _():
+            pltpu.make_async_copy(r1.at[k], r1.at[k], r1_sem.at[k]).wait()
+            total = rs[k].astype(F32)
+            for a in range(3):
+                total += r1[k, a].astype(F32)
+            r2s[k] = total.astype(BF16)
+            owner = owner_of(k)
+
+            @pl.when(owner == z)
+            def _():
+                r2[z // 4] = r2s[k]
+
+            @pl.when(owner != z)
+            def _():
+                pltpu.make_async_remote_copy(
+                    src_ref=r2s.at[k], dst_ref=r2.at[z // 4], send_sem=r2s_sem, recv_sem=r2_sem,
+                    device_id=(owner * X + x, d), device_id_type=MESH).start()
+
+        return carry
+
+    lax.fori_loop(0, OWN, level_two, 0)
 
     u = (d + 3 * z) % 8
     holds = u < 5
 
     @pl.when(holds)
     def _():
-        pltpu.make_async_copy(rr.at[0:Z - 1], rr.at[0:Z - 1], rr_sem).wait()
-        total = rr[0].astype(F32)
-        for a in range(1, Z):
-            total += rr[a].astype(F32)
+        pltpu.make_async_copy(r2.at[0:3], r2.at[0:3], r2_sem).wait()
+        total = r2[0].astype(F32)
+        for a in range(1, 4):
+            total += r2[a].astype(F32)
         total = total * 0.125
         for h in range(2):
             part = total[h * 80:(h + 1) * 80]
@@ -372,19 +427,25 @@
     def _():
         pltpu.make_async_copy(out_ref, out_ref, mr_sem).wait()
 
+    for stage, source in enumerate((zsa, zsb, zsc)):
+        pltpu.make_async_copy(source.at[0:Z - 1], source.at[0:Z - 1], zs_sem.at[stage]).wait()
     for j in range(PAIRS):
-        pltpu.make_async_copy(zs.at[j, 0:Z - 1], zs.at[j, 0:Z - 1], zs_sem).wait()
         pltpu.make_async_copy(xs.at[j, 0:X - 1], xs.at[j, 0:X - 1], xs_sem).wait()
     for stage, source in enumerate((psa, psb, psc)):
         pltpu.make_async_copy(source.at[0:GROUP - 1], source.at[0:GROUP - 1], ps_sem.at[stage]).wait()
 
-    @pl.when(holds)
-    def _():
-        pltpu.make_async_copy(rs.at[0:OWN - 1], rs.at[0:OWN - 1], rs_sem).wait()
-
-    @pl.when(jnp.logical_not(holds))
-    def _():
-        pltpu.make_async_copy(rs, rs, rs_sem).wait()
+    def sent(k, carry):
+        @pl.when(toward(k) != 0)
+        def _():
+            pltpu.make_async_copy(rs.at[k], rs.at[k], r1s_sem).wait()
+
+        @pl.when((toward(k) == 0) & (owner_of(k) != z))
+        def _():
+            pltpu.make_async_copy(r2s.at[k], r2s.at[k], r2s_sem).wait()
+
+        return carry
+
+    lax.fori_loop(0, OWN, sent, 0)
 
 
 def per_device(field, lon_count, wave_order, legendre):
@@ -392,31 +453,37 @@
     smem = pl.BlockSpec(memory_space=pltpu.SMEM)
     V = pltpu.VMEM
     scratch = [
+        V((LEV, LONS), BF16), V((2 * PAIRS, NLAT, M), BF16),
         V((LEV, LONS), BF16), V((2, 128, LONS), BF16), V((PAIRS, 4, 128, 128), F32),
-        V((PAIRS, Z, 16, LEV), BF16), V((PAIRS, Z, 16, LEV), BF16),
+        V((Z, 16, LEV), BF16), V((Z, 32, LEV), BF16), V((Z, 32, LEV), BF16),
+        V((Z, 16, LEV), BF16), V((Z, 32, LEV), BF16), V((Z, 32, LEV), BF16),
         V((PAIRS, X, 32, 256), BF16), V((PAIRS, X, 32, 256), BF16),
         V((256, 256), BF16), V((128, 128), BF16), V((1024, M), BF16), V((PAIRS, 128, M), BF16),
         V((PAIRS, 256, 128), BF16), V((PAIRS, 256, 128), BF16),
         V((PAIRS, 256, 128), BF16), V((PAIRS, 256, 128), BF16), V((PAIRS, 16, 128), BF16),
-        V((GROUP, 32, 256), BF16), V((GROUP, 48, 256), BF16), V((GROUP, 32, 256), BF16),
-        V((GROUP, 32, 256), BF16), V((GROUP, 48, 256), BF16), V((GROUP, 32, 256), BF16),
+        V((GROUP, 16, 256), BF16), V((GROUP, 48, 256), BF16), V((GROUP, 48, 256), BF16),
+        V((GROUP, 16, 256), BF16), V((GROUP, 48, 256), BF16), V((GROUP, 48, 256), BF16),
         V((7, 16, GROUP, 256), BF16), V((PAIRS, 32, 128), jnp.int32), V((OWN, 2, 128, 128), F32),
-        V((OWN, 160, 128), BF16), V((Z, 160, 128), BF16), V((D, 2, 16, 128), F32),
-        pltpu.SemaphoreType.DMA, pltpu.SemaphoreType.DMA((PAIRS,)),
+        V((OWN, 160, 128), BF16), V((OWN, 3, 160, 128), BF16), V((OWN, 160, 128), BF16),
+        V((4, 160, 128), BF16), V((D, 2, 16, 128), F32),
+        pltpu.SemaphoreType.DMA((2,)),
+        pltpu.SemaphoreType.DMA((3,)), pltpu.SemaphoreType.DMA((3,)),
         pltpu.SemaphoreType.DMA, pltpu.SemaphoreType.DMA((PAIRS,)),
         pltpu.SemaphoreType.DMA((3,)), pltpu.SemaphoreType.DMA((3,)),
+        pltpu.SemaphoreType.DMA, pltpu.SemaphoreType.DMA((OWN,)),
         pltpu.SemaphoreType.DMA, pltpu.SemaphoreType.DMA,
         pltpu.SemaphoreType.DMA, pltpu.SemaphoreType.DMA,
     ]
+    hbm = pl.BlockSpec(memory_space=pl.ANY)
     return pl.pallas_call(
         kernel,
         out_shape=jax.ShapeDtypeStruct((2, 5, 16, 128), F32),
-        in_specs=[smem, smem, vmem, vmem, vmem],
+        in_specs=[smem, smem, vmem, hbm, hbm],
         out_specs=vmem,
         scratch_shapes=scratch,
         compiler_params=pltpu.CompilerParams(
             collective_id=0, has_side_effects=True, vmem_limit_bytes=48 * 1024 * 1024),
-    )(lon_count, wave_order, wave_order.reshape(1, M), field.reshape(LEV, LONS), legendre)
+    )(lon_count, wave_order, wave_order, field.reshape(LEV, LONS), legendre)
 
 
 def solution(mesh):

time: 91.8 us -> 79.2 us (0.86)
  Pallas kernels: 87.3 us -> 74.7 us
    pallas_call x1, Pallas kernels: 87.3 us -> 74.7 us  [per_device(): pl.pallas_call(kernel, out_shape=jax.ShapeDtypeStruct((2, 5, 16, 128), F3...]
where the time goes in v2:
time: 79.2 us; the launch traced here: 79 us
  Pallas kernels  74.7 us (94%)
  local copies, waits for them, and re-layouts  3.56 us (4%)
    pallas_call x1, Pallas kernels, per_device(): pl.pallas_call(kernel, out_shape=jax.ShapeDtypeStruct((2, 5, 16, 128), F3...  74.7 us
    unnamed x7, local copies, waits for them, and re-layouts  3.56 us

profile of v2, /device:TPU:1, one launch (start us, length us, event | category | flops | bytes accessed | tf_op | source)
XLA Modules:
  0.0 79.0 jit_solution(6557734903570126099)
XLA Ops:
  0.7 0.0 copy-start
  0.7 1.1 %copy-done = bf16[10,64,640]{2,1,0:T(8,128)(2,1)S(1)} copy-done((bf16[10,64,640]{2,1,0:T(8,128)(2,1)S(1)}, bf16[10,64,640]{2,1,0:T(8,128)(2,1)}, u32[]{:S(2)}) %copy-start) | copy-done | bytes 819224
  1.8 0.0 copy-start.1
  1.8 1.1 %copy-done.1 = bf16[1,1,128,2688]{3,2,1,0:T(8,128)(2,1)S(1)} copy-done((bf16[1,1,128,2688]{3,2,1,0:T(8,128)(2,1)S(1)}, bf16[1,1,128,2688]{3,2,1,0:T(8,128)(2,1)}, u32[]{:S(2)}) %copy-start.1) | copy-done | bytes 688152
  2.9 0.0 copy-start.2
  2.9 0.7 copy-done.2
  3.6 74.7 %shard_map.46 = f32[2,5,16,128]{3,2,1,0:T(8,128)S(1)} custom-call(s32[1]{0:T(128)S(6)} %copy.6.count_ref, s32[640]{0:T(1024)S(1)} %copy-done.2, s32[640]{0:T(1024)S(1)} %copy-done.2, bf16[128,2688]{1,0:T(8,128)(2,1)S(1)} %bitcast.1, bf16[10,64,640]{2,1,0:T(8,128)(2,1)S(1)} %copy-done), custom_call_target="tpu_custom_call" | custom-call | tf_op jit(solution)/shard_map/pallas_call | solution.py:478
  78.3 0.6 copy.7
Async XLA Ops:
  0.7 1.1 %copy-start = (bf16[10,64,640]{2,1,0:T(8,128)(2,1)S(1)}, bf16[10,64,640]{2,1,0:T(8,128)(2,1)}, u32[]{:S(2)}) copy-start(bf16[10,64,640]{2,1,0:T(8,128)(2,1)} %leg_ref.1) | copy-start | bytes 2457604
  1.8 1.1 %copy-start.1 = (bf16[1,1,128,2688]{3,2,1,0:T(8,128)(2,1)S(1)}, bf16[1,1,128,2688]{3,2,1,0:T(8,128)(2,1)}, u32[]{:S(2)}) copy-start(bf16[1,1,128,2688]{3,2,1,0:T(8,128)(2,1)} %param.4) | copy-start | bytes 2064388
  2.9 0.7 copy-start.2

commit v3 on v2

v3 whole, which is shorter than its diff:
```python
import jax
import jax.numpy as jnp
from jax import lax
from jax.experimental import pallas as pl
from jax.experimental.pallas import tpu as pltpu
from jax.sharding import PartitionSpec as P

MESH = pl.DeviceIdType.MESH
F32 = jnp.float32
BF16 = jnp.bfloat16
Z, X, D = 16, 4, 8
GROUP = X * D
LEV, LONS, M, NLAT = 128, 2688, 640, 64
PAIRS = 5
EXTRA = (6, 7, 14, 4, 5)
OWN = 10
COS = (1.0, -19.739208221435547, 64.93939208984375, -85.45681762695312, 60.24457931518555,
       -26.425565719604492, 7.898900985717773, -1.6961979866027832, 0.24304766952991486)
SIN = (6.2831854820251465, -41.34170150756836, 81.6052474975586, -76.70585632324219, 42.05867385864258,
       -15.094411849975586, 3.818404197692871, -0.7120527029037476, 0.09126123040914536)


STEPS = sorted(((dx, dy, dc) for dx in range(4) for dy in range(4) for dc in range(2) if dx or dy or dc),
               key=lambda s: -min(s[0], 4 - s[0]) - min(s[1], 4 - s[1]))


def iota(shape, dim):
    return lax.broadcasted_iota(jnp.int32, shape, dim)


def dot(a, b, ca, cb):
    return lax.dot_general(a, b, (((ca,), (cb,)), ((), ())), preferred_element_type=F32)


def poly(coefficients, v):
    total = jnp.full_like(v, coefficients[-1])
    for value in coefficients[-2::-1]:
        total = total * v + value
    return total


def unit(product, count, inverse):
    turns = jnp.floor(product * inverse + 0.5)
    u = (product - turns * count) * inverse
    v = u * u
    return poly(COS, v), -u * poly(SIN, v)


def one_hot(condition):
    return jnp.where(condition, 1.0, 0.0).astype(BF16)


def total_wave(dest, k):
    t = (dest & 7) + 8 * k
    zz = (t * 205) >> 10
    return 20 * zz + 5 * (dest >> 3) + (t - 5 * zz)


def kernel(count_ref, wave_ref, waves_ref, field_ref, leg_ref, out_ref,
           fi, li, fm, tbl, base, xs, xg, zs0, zs1, zs2, zs3, zr0, zr1, zr2, zr3, xr, p256, pz, prow, pcol, lr, lu, lv, lul, lvl, lw,
           ps0, ps1, ps2, ps3, ps4, ps5, pr0, pr1, pr2, pr3, pr4, pr5, ab, mt, acc, rs, r1, r2s, r2,
           in_sem, zs_sem, zr_sem, xs_sem, xr_sem, ps_sem, pr_sem, r1s_sem, r1_sem, r2s_sem, r2_sem):
    field_in = pltpu.make_async_copy(field_ref, fi, in_sem.at[0])
    leg_in = pltpu.make_async_copy(leg_ref, li, in_sem.at[1])
    field_in.start()
    leg_in.start()
    lat = lax.axis_index("lat")
    d = lax.axis_index("mem")
    z, x = lat // X, lat % X
    me = x * D + d

    def z_partner(o):
        far = 8 - (o + 1) // 2
        other = (z + far + (1 - o % 2) * (Z - 2 * far)) % Z
        return other, (other * X + x, d)

    def plane_partner(step):
        other_x = (x + step[0]) % X
        other_d = (d // 2 + step[1]) % 4 * 2 + (d + step[2]) % 2
        return other_x * D + other_d, (z * X + other_x, other_d)

    barrier = pltpu.get_barrier_semaphore()

    def greet_z(o, carry):
        pl.semaphore_signal(barrier, inc=1, device_id=z_partner(o)[1], device_id_type=MESH)
        return carry

    lax.fori_loop(0, Z - 1, greet_z, 0)
    for step in STEPS:
        pl.semaphore_signal(barrier, inc=1, device_id=plane_partner(step)[1], device_id_type=MESH)

    count = count_ref[0].astype(F32)
    inverse = 1.0 / jnp.full((128, 128), count, F32)
    wave_row = waves_ref[...].astype(F32).reshape(1, M)
    p_row = iota((128, M), 0)

    def make_base(j, carry):
        slot = 10 * (4 * ((p_row >> 1) & 15) + (p_row >> 5)) + 2 * j + (p_row & 1)
        wave = jnp.sum(jnp.where(iota((128, M), 1) == slot, wave_row, 0.0), axis=1, keepdims=True)
        wave = jnp.broadcast_to(wave, (128, 128))
        c, s = unit(wave * iota((128, 128), 1).astype(F32), count, inverse)
        base[j, 0] = c
        base[j, 1] = s
        c, s = unit(wave * 128.0, count, inverse)
        base[j, 2] = c
        base[j, 3] = s
        return carry

    lax.fori_loop(0, PAIRS, make_base, 0)
    o_row, o_col = iota((256, 256), 0), iota((256, 256), 1)
    p256[...] = one_hot(o_col == (o_row & 15) * 16 + (o_row >> 4))
    pz[...] = one_hot(o_col == ((o_row >> 2) & 3) * 64 + ((o_row >> 1) & 1) * 32 + (o_row >> 4) * 2 + (o_row & 1))
    field_in.wait()
    fm[...] = jnp.where(iota((LEV, LONS), 1) < count_ref[0], fi[...].astype(F32), 0.0).astype(BF16)

    def transform(j):
        def rows(b, inner):
            at = pl.ds(pl.multiple_of(b * 32, 32), 32)
            c, s = base[j, 0, at, :], base[j, 1, at, :]
            cw, sw = base[j, 2, at, :], base[j, 3, at, :]
            for a in range(LONS // 128):
                tbl[0, at, a * 128:(a + 1) * 128] = c.astype(BF16)
                tbl[1, at, a * 128:(a + 1) * 128] = s.astype(BF16)
                c, s = c * cw - s * sw, c * sw + s * cw
            return inner

        lax.fori_loop(0, 4, rows, 0)
        summed = dot(tbl[...].reshape(256, LONS), fm[...], 1, 1) / count
        for xx in range(X):
            at = xx * 32
            xs[j, xx] = jnp.concatenate([summed[at:at + 32], summed[128 + at:160 + at]], axis=0).astype(BF16)

    def send_x(j):
        xg[j, x] = xs[j, x]

        def send(o, carry):
            other = (x + o) % X
            pltpu.make_async_remote_copy(
                src_ref=xs.at[j, other], dst_ref=xg.at[j, x], send_sem=xs_sem, recv_sem=xr_sem.at[j],
                device_id=(z * X + other, d), device_id_type=MESH).start()
            return carry

        lax.fori_loop(1, X, send, 0)

    def pass_on(j, target, place):
        pltpu.make_async_copy(xg.at[j, 0:X - 1], xg.at[j, 0:X - 1], xr_sem.at[j]).wait()
        moved = dot(pz[...], xg[j].reshape(256, LEV), 1, 0).astype(BF16)
        target[:, place:place + 16, :] = moved.reshape(Z, 16, LEV)

    def send_z(stage, source, target):
        target[z] = source[z]

        def send(o, carry):
            other, device = z_partner(o)
            pltpu.make_async_remote_copy(
                src_ref=source.at[other], dst_ref=target.at[z], send_sem=zs_sem.at[stage],
                recv_sem=zr_sem.at[stage], device_id=device, device_id_type=MESH).start()
            return carry

        lax.fori_loop(0, Z - 1, send, 0)

    transform(0)
    pl.semaphore_wait(barrier, Z - 1 + GROUP - 1)
    send_x(0)
    transform(1)
    send_x(1)
    pass_on(0, zs0, 0)
    send_z(0, zs0, zr0)
    transform(2)
    send_x(2)
    pass_on(1, zs1, 0)
    send_z(1, zs1, zr1)
    transform(3)
    send_x(3)
    pass_on(2, zs2, 0)
    send_z(2, zs2, zr2)
    transform(4)
    send_x(4)
    pass_on(3, zs3, 0)
    pass_on(4, zs3, 16)
    send_z(3, zs3, zr3)

    o_row, o_col = iota((128, 128), 0), iota((128, 128), 1)
    prow[...] = one_hot(o_col == ((o_row >> 4) & 1) * 64 + 4 * (o_row & 15) + (o_row >> 5))
    c_row = iota((256, 1), 0)
    i_main = total_wave(c_row >> 3, c_row & 7)
    i_left = total_wave(c_row >> 3, 8 + (c_row & 1))
    n_col = iota((256, M), 1)
    pcol[0:256] = one_hot(n_col == M - 1 - i_main)
    pcol[256:512] = one_hot(n_col == i_main)
    pcol[512:768] = one_hot(n_col == M - 1 - i_left)
    pcol[768:1024] = one_hot(n_col == i_left)

    lane_slot = (iota((1, 128), 1) >> 4) & 1
    left_j = (c_row >> 1) & 3

    def legendre(j):
        lr[j] = dot(prow[...], li[2 * j:2 * j + 2].reshape(128, M), 1, 0).astype(BF16)
        w0 = wave_ref[10 * lat + 2 * j]
        w1 = wave_ref[10 * lat + 2 * j + 1]
        low = jnp.minimum(w0, w1)
        small = jnp.where(lane_slot == 0, w0, w1) == low
        put = pcol[...]
        moved = dot(put, lr[j], 1, 1)
        upper, lower, upper_left, lower_left = (moved[a * 256:(a + 1) * 256] for a in range(4))
        high = jnp.where(small, upper, 0.0)
        deep = jnp.where(small, jnp.where(i_main >= low, lower, 0.0), jnp.where(i_main < low, upper, 0.0))
        if j >= 3:
            high, deep = high.reshape(GROUP, 8, 128), deep.reshape(GROUP, 8, 128)
            high, deep = (jnp.concatenate([high[:, a:a + 4], deep[:, a:a + 4]], axis=1).reshape(256, 128) for a in (0, 4))
        lu[j] = high.astype(BF16)
        lv[j] = deep.astype(BF16)
        here = left_j == j % 3
        lul[j] = jnp.where(here & small, upper_left, 0.0).astype(BF16)
        lvl[j] = jnp.where(small, jnp.where(here & (i_left >= low), lower_left, 0.0),
                           jnp.where(here & (i_left < low), upper_left, 0.0)).astype(BF16)
        pick = one_hot((iota((16, M), 0) == EXTRA[j]) & (iota((16, M), 1) == M - 1 - low))
        lw[j] = jnp.where(small, 0.0, dot(pick, lr[j], 1, 1)).astype(BF16)
        for xx in range(X):
            wave = wave_ref[10 * (X * z + xx) + 2 * j]
            mt[j, xx * 8:(xx + 1) * 8, :] = jnp.full((8, 128), jnp.minimum(wave, M - 1 - wave), jnp.int32)

    def rows_along_z(stage, source):
        pltpu.make_async_copy(source.at[0:Z - 1], source.at[0:Z - 1], zr_sem.at[stage]).wait()

    def gather(j, source, place):
        piece = source[:, place:place + 16, :].reshape(256, LEV)
        moved = dot(p256[...], piece, 1, 0).astype(BF16)
        for xx in range(X):
            for q in range(2):
                at = (xx * 4 + q * 2) * 16
                xr[j, xx, :, q * 128:(q + 1) * 128] = moved[at:at + 32]

    def both_kinds(up, low):
        return jnp.concatenate([up.reshape(GROUP, 8, 256), low.reshape(GROUP, 8, 256)], axis=1).astype(BF16)

    def spectral(j, target, place):
        rhs = xr[j].reshape(128, 256)
        target[:, place:place + 16, :] = both_kinds(dot(lu[j], rhs, 1, 0), dot(lv[j], rhs, 1, 0))

    def send_plane(stage, source, target):
        target[me] = source[me]

        for step in STEPS:
            other, device = plane_partner(step)
            pltpu.make_async_remote_copy(
                src_ref=source.at[other], dst_ref=target.at[me], send_sem=ps_sem.at[stage],
                recv_sem=pr_sem.at[stage], device_id=device, device_id_type=MESH).start()

    def left_over(js, target, place):
        up, low = jnp.zeros((256, 256), F32), jnp.zeros((256, 256), F32)
        extra = jnp.zeros((16, 256), F32)
        for j in js:
            rhs = xr[j].reshape(128, 256)
            up += dot(lul[j], rhs, 1, 0)
            low += dot(lvl[j], rhs, 1, 0)
            extra += dot(lw[j], rhs, 1, 0)
        up = up.reshape(GROUP, 8, 256) + extra[0:8][None]
        low = low.reshape(GROUP, 8, 256) + extra[8:16][None]
        target[:, place:place + 16, :] = both_kinds(up, low)

    leg_in.wait()
    legendre(0)
    rows_along_z(0, zr0)
    gather(0, zr0, 0)
    spectral(0, ps0, 0)
    send_plane(0, ps0, pr0)
    legendre(1)
    rows_along_z(1, zr1)
    gather(1, zr1, 0)
    spectral(1, ps1, 0)
    send_plane(1, ps1, pr1)
    legendre(2)
    rows_along_z(2, zr2)
    gather(2, zr2, 0)
    spectral(2, ps2, 0)
    left_over((0, 1, 2), ps2, 16)
    send_plane(2, ps2, pr2)
    legendre(3)
    legendre(4)

    def arrived(stage, target, subs):
        pltpu.make_async_copy(target.at[0:GROUP - 1], target.at[0:GROUP - 1], pr_sem.at[stage]).wait()
        for b, sub in enumerate(subs):
            for g in range(2):
                piece = target[g * 16:(g + 1) * 16, b * 16:(b + 1) * 16, :].reshape(256, 256)
                moved = dot(p256[...], piece, 1, 0).astype(BF16)
                ab[sub, :, g * 16:(g + 1) * 16, :] = moved.reshape(16, 16, 256)

    def halves(rows):
        return jnp.concatenate([rows[:, 0:128], rows[:, 128:256]], axis=0)

    def waves_of(js):
        tile = jnp.concatenate([mt[j] for j in js], axis=0)
        return jnp.concatenate([tile, tile], axis=0)

    def gram(k, ups, lows, js, first, extras=None, extra_js=()):
        i = total_wave(me, k)
        up = halves(jnp.concatenate(ups, axis=0))
        low = halves(jnp.concatenate(lows, axis=0))
        waves = waves_of(js)
        inside = low * one_hot(waves <= i)
        outside = low * one_hot(waves > i)
        near = dot(low, inside, 0, 0)
        far = dot(up, up, 0, 0) + dot(low, outside, 0, 0)
        if extras is not None:
            far += dot(extras, extras * one_hot(waves_of(extra_js) == i), 0, 0)
        if first:
            acc[k, 0] = near
            acc[k, 1] = far
        else:
            acc[k, 0] += near
            acc[k, 1] += far

    arrived(0, pr0, (0,))

    def gram_a(k, carry):
        gram(k, [ab[0, k]], [ab[0, 8 + k]], (0,), True)
        return carry

    lax.fori_loop(0, 8, gram_a, 0)

    rows_along_z(3, zr3)
    gather(3, zr3, 0)
    gather(4, zr3, 16)
    left_over((3, 4), ps3, 0)
    send_plane(3, ps3, pr3)
    rhs3, rhs4 = xr[3].reshape(128, 256), xr[4].reshape(128, 256)
    ps4[...] = both_kinds(dot(lu[3], rhs3, 1, 0), dot(lu[4], rhs4, 1, 0))
    send_plane(4, ps4, pr4)
    ps5[...] = both_kinds(dot(lv[3], rhs3, 1, 0), dot(lv[4], rhs4, 1, 0))
    send_plane(5, ps5, pr5)

    arrived(1, pr1, (1,))
    arrived(2, pr2, (2, 5))
    extras_b = halves(jnp.concatenate([ab[5, EXTRA[j]] for j in (0, 1, 2)], axis=0))

    def gram_b(k, carry):
        gram(k, [ab[1, k], ab[2, k]], [ab[1, 8 + k], ab[2, 8 + k]], (1, 2), False, extras_b, (0, 1, 2))
        return carry

    lax.fori_loop(0, 8, gram_b, 0)
    for kk in range(2):
        gram(8 + kk, [ab[5, 2 * j + kk] for j in range(3)], [ab[5, 8 + 2 * j + kk] for j in range(3)],
             (0, 1, 2), True, extras_b, (0, 1, 2))

    lane = iota((16, 128), 1)

    behind = 1 + d % 2

    def owner_of(k):
        return (d + 8 * k) // 5

    def toward(k):
        return (owner_of(k) - z + Z + behind) % 4 - behind

    def pack_send(k):
        for h in range(2):
            whole = acc[k, h]
            blocks = [whole[0:16]]
            for r in range(1, 4):
                folded = pltpu.roll(whole[16 * (8 - r):16 * (9 - r)], 16 * r, 1)
                blocks.append(jnp.where(lane >= 16 * r, whole[16 * r:16 * (r + 1)], folded))
            blocks.append(whole[64:80])
            rs[k, h * 80:(h + 1) * 80, :] = jnp.concatenate(blocks, axis=0).astype(BF16)
        step = toward(k)
        seat = step + behind

        @pl.when(step != 0)
        def _():
            pltpu.make_async_remote_copy(
                src_ref=rs.at[k], dst_ref=r1.at[k, seat - (seat + 3 - behind) // 4], send_sem=r1s_sem,
                recv_sem=r1_sem.at[k], device_id=(((z + step + Z) % Z) * X + x, d), device_id_type=MESH).start()

    keep = (iota((128, 128), 1) >> 4) >= (iota((128, 128), 0) >> 4)

    def level_two(k, carry):
        @pl.when(toward(k) == 0)
        def _():
            pltpu.make_async_copy(r1.at[k], r1.at[k], r1_sem.at[k]).wait()
            total = rs[k].astype(F32)
            for a in range(3):
                total += r1[k, a].astype(F32)
            for h in range(2):
                part = total[h * 80:(h + 1) * 80]
                blocks = [part[16 * r:16 * (r + 1)] for r in range(5)]
                for r in range(3, 0, -1):
                    blocks.append(pltpu.roll(part[16 * r:16 * (r + 1)], 128 - 16 * r, 1))
                upper = jnp.concatenate(blocks, axis=0)
                r2s[k, :, h] = jnp.where(keep, upper, upper.T).astype(BF16).reshape(D, 16, 128)
            owner = owner_of(k)
            seat = (d + 8 * k) % 5 * 4 + z // 4

            def send(o, inner):
                other = (d + o) % D
                pltpu.make_async_remote_copy(
                    src_ref=r2s.at[k, other], dst_ref=r2.at[seat], send_sem=r2s_sem, recv_sem=r2_sem,
                    device_id=(owner * X + x, other), device_id_type=MESH).start()
                return inner

            lax.fori_loop(1, D, send, 0)

            @pl.when(owner == z)
            def _():
                r2[seat] = r2s[k, d]

            @pl.when(owner != z)
            def _():
                send(0, 0)

        return carry

    arrived(3, pr3, (6,))
    extras_c = halves(jnp.concatenate([ab[6, EXTRA[j]] for j in (3, 4)], axis=0))

    def gram_left(kk, carry):
        gram(8 + kk, [ab[6, kk], ab[6, 2 + kk]], [ab[6, 8 + kk], ab[6, 10 + kk]], (3, 4), False, extras_c, (3, 4))
        pack_send(8 + kk)
        return carry

    lax.fori_loop(0, 2, gram_left, 0)
    for half, (source, sub) in enumerate(((pr4, 3), (pr5, 4))):
        arrived(4 + half, source, (sub,))

        def gram_c(k, carry, sub=sub, half=half):
            gram(4 * half + k, [ab[sub, k], ab[sub, 8 + k]], [ab[sub, 4 + k], ab[sub, 12 + k]], (3, 4), False,
                 extras_c, (3, 4))
            pack_send(4 * half + k)
            return carry

        lax.fori_loop(0, 4, gram_c, 0)
        if half == 0:
            lax.fori_loop(8, OWN, level_two, 0)

    lax.fori_loop(0, 4, level_two, 0)
    lax.fori_loop(4, 8, level_two, 0)
    holds = (d + 3 * z) % 8 < 5

    @pl.when(holds)
    def _():
        pltpu.make_async_copy(r2.at[0:19], r2.at[0:19], r2_sem).wait()

    @pl.when(jnp.logical_not(holds))
    def _():
        pltpu.make_async_copy(r2, r2, r2_sem).wait()

    for u in range(5):
        total = r2[4 * u].astype(F32)
        for a in range(1, 4):
            total += r2[4 * u + a].astype(F32)
        out_ref[:, u] = total * 0.125

    for stage, source in enumerate((zs0, zs1, zs2, zs3)):
        pltpu.make_async_copy(source.at[0:Z - 1], source.at[0:Z - 1], zs_sem.at[stage]).wait()
    for j in range(PAIRS):
        pltpu.make_async_copy(xs.at[j, 0:X - 1], xs.at[j, 0:X - 1], xs_sem).wait()
    for stage, source in enumerate((ps0, ps1, ps2, ps3, ps4, ps5)):
        pltpu.make_async_copy(source.at[0:GROUP - 1], source.at[0:GROUP - 1], ps_sem.at[stage]).wait()

    def sent(k, carry):
        @pl.when(toward(k) != 0)
        def _():
            pltpu.make_async_copy(rs.at[k], rs.at[k], r1s_sem).wait()

        @pl.when((toward(k) == 0) & (owner_of(k) != z))
        def _():
            pltpu.make_async_copy(r2s.at[k], r2s.at[k], r2s_sem).wait()

        @pl.when(owner_of(k) == z)
        def _():
            pltpu.make_async_copy(r2s.at[k, 0:D - 1], r2s.at[k, 0:D - 1], r2s_sem).wait()

        return carry

    lax.fori_loop(0, OWN, sent, 0)


def per_device(field, lon_count, wave_order, legendre):
    vmem = pl.BlockSpec(memory_space=pltpu.VMEM)
    smem = pl.BlockSpec(memory_space=pltpu.SMEM)
    V = pltpu.VMEM
    scratch = [
        V((LEV, LONS), BF16), V((2 * PAIRS, NLAT, M), BF16),
        V((LEV, LONS), BF16), V((2, 128, LONS), BF16), V((PAIRS, 4, 128, 128), F32),
        V((PAIRS, X, 64, LEV), BF16), V((PAIRS, X, 64, LEV), BF16),
        *[V((Z, rows, LEV), BF16) for rows in (16, 16, 16, 32)] * 2, V((PAIRS, X, 32, 256), BF16), V((256, 256), BF16),
        V((256, 256), BF16), V((128, 128), BF16), V((1024, M), BF16), V((PAIRS, 128, M), BF16),
        V((PAIRS, 256, 128), BF16), V((PAIRS, 256, 128), BF16),
        V((PAIRS, 256, 128), BF16), V((PAIRS, 256, 128), BF16), V((PAIRS, 16, 128), BF16),
        *[V((GROUP, rows, 256), BF16) for rows in (16, 16, 32, 16, 16, 16)] * 2,
        V((7, 16, GROUP, 256), BF16), V((PAIRS, 32, 128), jnp.int32), V((OWN, 2, 128, 128), F32),
        V((OWN, 160, 128), BF16), V((OWN, 3, 160, 128), BF16), V((OWN, D, 2, 16, 128), BF16),
        V((20, 2, 16, 128), BF16),
        pltpu.SemaphoreType.DMA((2,)),
        pltpu.SemaphoreType.DMA((4,)), pltpu.SemaphoreType.DMA((4,)),
        pltpu.SemaphoreType.DMA, pltpu.SemaphoreType.DMA((PAIRS,)),
        pltpu.SemaphoreType.DMA((6,)), pltpu.SemaphoreType.DMA((6,)),
        pltpu.SemaphoreType.DMA, pltpu.SemaphoreType.DMA((OWN,)),
        pltpu.SemaphoreType.DMA, pltpu.SemaphoreType.DMA,
    ]
    hbm = pl.BlockSpec(memory_space=pltpu.HBM)
    return pl.pallas_call(
        kernel,
        out_shape=jax.ShapeDtypeStruct((2, 5, 16, 128), F32),
        in_specs=[smem, smem, vmem, hbm, hbm],
        out_specs=vmem,
        scratch_shapes=scratch,
        compiler_params=pltpu.CompilerParams(
            collective_id=0, has_side_effects=True, vmem_limit_bytes=60 * 1024 * 1024),
    )(lon_count, wave_order, wave_order, field.reshape(LEV, LONS), legendre)


def solution(mesh):
    return jax.shard_map(
        per_device,
        mesh=mesh,
        in_specs=(P("mem", "lat", None, None), P("lat"), P(), P("lat", None, None)),
        out_specs=P(None, "lat", "mem", None),
        check_vma=False,
    )
```

time: 79.2 us -> 75.9 us (0.958)
  local copies, waits for them, and re-layouts: 3.56 us -> 1.53 us
  Pallas kernels: 74.7 us -> 73.6 us
    unnamed x7 -> x1, local copies, waits for them, and re-layouts: 3.56 us -> 1.53 us
    pallas_call x1, Pallas kernels: 74.7 us -> 73.6 us  [per_device(): pl.pallas_call(kernel, out_shape=jax.ShapeDtypeStruct((2, 5, 16, 128), F3...]
where the time goes in v3:
time: 75.9 us; the launch traced here: 75.8 us
  Pallas kernels  73.6 us (97%)
  local copies, waits for them, and re-layouts  1.53 us (2%)
    pallas_call x1, Pallas kernels, per_device(): pl.pallas_call(kernel, out_shape=jax.ShapeDtypeStruct((2, 5, 16, 128), F3...  73.6 us
    unnamed x1, local copies, waits for them, and re-layouts  1.53 us

profile of v3, /device:TPU:1, one launch (start us, length us, event | category | flops | bytes accessed | tf_op | source)
XLA Modules:
  0.0 75.8 jit_solution(13302078974043960871)
XLA Ops:
  0.7 73.6 %shard_map.46 = f32[2,5,16,128]{3,2,1,0:T(8,128)} custom-call(s32[1]{0:T(128)S(6)} %copy.6.count_ref, s32[640]{0:T(1024)} %waves_ref.1, s32[640]{0:T(1024)} %waves_ref.1, bf16[128,2688]{1,0:T(8,128)(2,1)} %bitcast.1, bf16[10,64,640]{2,1,0:T(8,128)(2,1)} %leg_ref.1), custom_call_target="tpu_custom_call" | custom-call | tf_op jit(solution)/shard_map/pallas_call | solution.py:502
  74.2 1.5 %copy.7 = f32[2,5,16,128]{3,2,1,0:T(8,128)} copy(f32[2,5,16,128]{3,2,1,0:T(8,128)} %shard_map.46) | data formatting | bytes 163840

commit v4 on v3

--- a/solution.py
+++ b/solution.py
@@ -81,13 +81,12 @@
 
     barrier = pltpu.get_barrier_semaphore()
 
-    def greet_z(o, carry):
+    for o in range(Z - 1):
         pl.semaphore_signal(barrier, inc=1, device_id=z_partner(o)[1], device_id_type=MESH)
-        return carry
-
-    lax.fori_loop(0, Z - 1, greet_z, 0)
-    for step in STEPS:
-        pl.semaphore_signal(barrier, inc=1, device_id=plane_partner(step)[1], device_id_type=MESH)
+    for o in range(1, X):
+        pl.semaphore_signal(barrier, inc=1, device_id=(z * X + (x + o) % X, d), device_id_type=MESH)
+    for o in range(1, D):
+        pl.semaphore_signal(barrier, inc=1, device_id=(lat, (d + o) % D), device_id_type=MESH)
 
     count = count_ref[0].astype(F32)
     inverse = 1.0 / jnp.full((128, 128), count, F32)
@@ -106,10 +105,7 @@
         base[j, 3] = s
         return carry
 
-    lax.fori_loop(0, PAIRS, make_base, 0)
-    o_row, o_col = iota((256, 256), 0), iota((256, 256), 1)
-    p256[...] = one_hot(o_col == (o_row & 15) * 16 + (o_row >> 4))
-    pz[...] = one_hot(o_col == ((o_row >> 2) & 3) * 64 + ((o_row >> 1) & 1) * 32 + (o_row >> 4) * 2 + (o_row & 1))
+    make_base(0, 0)
     field_in.wait()
     fm[...] = jnp.where(iota((LEV, LONS), 1) < count_ref[0], fi[...].astype(F32), 0.0).astype(BF16)
 
@@ -133,14 +129,11 @@
     def send_x(j):
         xg[j, x] = xs[j, x]
 
-        def send(o, carry):
+        for o in range(1, X):
             other = (x + o) % X
             pltpu.make_async_remote_copy(
                 src_ref=xs.at[j, other], dst_ref=xg.at[j, x], send_sem=xs_sem, recv_sem=xr_sem.at[j],
                 device_id=(z * X + other, d), device_id_type=MESH).start()
-            return carry
-
-        lax.fori_loop(1, X, send, 0)
 
     def pass_on(j, target, place):
         pltpu.make_async_copy(xg.at[j, 0:X - 1], xg.at[j, 0:X - 1], xr_sem.at[j]).wait()
@@ -150,18 +143,19 @@
     def send_z(stage, source, target):
         target[z] = source[z]
 
-        def send(o, carry):
+        for o in range(Z - 1):
             other, device = z_partner(o)
             pltpu.make_async_remote_copy(
                 src_ref=source.at[other], dst_ref=target.at[z], send_sem=zs_sem.at[stage],
                 recv_sem=zr_sem.at[stage], device_id=device, device_id_type=MESH).start()
-            return carry
-
-        lax.fori_loop(0, Z - 1, send, 0)
 
     transform(0)
-    pl.semaphore_wait(barrier, Z - 1 + GROUP - 1)
+    pl.semaphore_wait(barrier, Z - 1 + X - 1 + D - 1)
     send_x(0)
+    lax.fori_loop(1, PAIRS, make_base, 0)
+    o_row, o_col = iota((256, 256), 0), iota((256, 256), 1)
+    p256[...] = one_hot(o_col == (o_row & 15) * 16 + (o_row >> 4))
+    pz[...] = one_hot(o_col == ((o_row >> 2) & 3) * 64 + ((o_row >> 1) & 1) * 32 + (o_row >> 4) * 2 + (o_row & 1))
     transform(1)
     send_x(1)
     pass_on(0, zs0, 0)
@@ -172,10 +166,10 @@
     send_z(1, zs1, zr1)
     transform(3)
     send_x(3)
+    transform(4)
+    send_x(4)
     pass_on(2, zs2, 0)
     send_z(2, zs2, zr2)
-    transform(4)
-    send_x(4)
     pass_on(3, zs3, 0)
     pass_on(4, zs3, 16)
     send_z(3, zs3, zr3)
@@ -279,8 +273,10 @@
     legendre(3)
     legendre(4)
 
-    def arrived(stage, target, subs):
+    def arrived(stage, target, subs, then=None):
         pltpu.make_async_copy(target.at[0:GROUP - 1], target.at[0:GROUP - 1], pr_sem.at[stage]).wait()
+        if then is not None:
+            send_plane(*then)
         for b, sub in enumerate(subs):
             for g in range(2):
                 piece = target[g * 16:(g + 1) * 16, b * 16:(b + 1) * 16, :].reshape(256, 256)
@@ -327,12 +323,10 @@
     send_plane(3, ps3, pr3)
     rhs3, rhs4 = xr[3].reshape(128, 256), xr[4].reshape(128, 256)
     ps4[...] = both_kinds(dot(lu[3], rhs3, 1, 0), dot(lu[4], rhs4, 1, 0))
-    send_plane(4, ps4, pr4)
     ps5[...] = both_kinds(dot(lv[3], rhs3, 1, 0), dot(lv[4], rhs4, 1, 0))
-    send_plane(5, ps5, pr5)
 
     arrived(1, pr1, (1,))
-    arrived(2, pr2, (2, 5))
+    arrived(2, pr2, (2, 5), (4, ps4, pr4))
     extras_b = halves(jnp.concatenate([ab[5, EXTRA[j]] for j in (0, 1, 2)], axis=0))
 
     def gram_b(k, carry):
@@ -391,14 +385,14 @@
             owner = owner_of(k)
             seat = (d + 8 * k) % 5 * 4 + z // 4
 
-            def send(o, inner):
+            def send(o):
                 other = (d + o) % D
                 pltpu.make_async_remote_copy(
                     src_ref=r2s.at[k, other], dst_ref=r2.at[seat], send_sem=r2s_sem, recv_sem=r2_sem,
                     device_id=(owner * X + x, other), device_id_type=MESH).start()
-                return inner
-
-            lax.fori_loop(1, D, send, 0)
+
+            for o in range(1, D):
+                send(o)
 
             @pl.when(owner == z)
             def _():
@@ -406,11 +400,11 @@
 
             @pl.when(owner != z)
             def _():
-                send(0, 0)
+                send(0)
 
         return carry
 
-    arrived(3, pr3, (6,))
+    arrived(3, pr3, (6,), (5, ps5, pr5))
     extras_c = halves(jnp.concatenate([ab[6, EXTRA[j]] for j in (3, 4)], axis=0))
 
     def gram_left(kk, carry):

time: 75.9 us -> 73.1 us (0.963); the launches traced: 75.8 us -> 71.9 us
  Pallas kernels: 73.6 us -> 69.7 us
    pallas_call x1, Pallas kernels: 73.6 us -> 69.7 us  [per_device(): pl.pallas_call(kernel, out_shape=jax.ShapeDtypeStruct((2, 5, 16, 128), F3...]
where the time goes in v4:
time: 73.1 us; the launch traced here: 71.9 us
  Pallas kernels  69.7 us (95%)
  local copies, waits for them, and re-layouts  1.53 us (2%)
    pallas_call x1, Pallas kernels, per_device(): pl.pallas_call(kernel, out_shape=jax.ShapeDtypeStruct((2, 5, 16, 128), F3...  69.7 us
    unnamed x1, local copies, waits for them, and re-layouts  1.53 us

profile of v4, /device:TPU:1, one launch (start us, length us, event | category | flops | bytes accessed | tf_op | source)
XLA Modules:
  0.0 71.9 jit_solution(3015629364517293564)
XLA Ops:
  0.7 69.7 %shard_map.46 = f32[2,5,16,128]{3,2,1,0:T(8,128)} custom-call(s32[1]{0:T(128)S(6)} %copy.6.count_ref, s32[640]{0:T(1024)} %waves_ref.1, s32[640]{0:T(1024)} %waves_ref.1, bf16[128,2688]{1,0:T(8,128)(2,1)} %bitcast.1, bf16[10,64,640]{2,1,0:T(8,128)(2,1)} %leg_ref.1), custom_call_target="tpu_custom_call" | custom-call | tf_op jit(solution)/shard_map/pallas_call | solution.py:496
  70.3 1.5 %copy.7 = f32[2,5,16,128]{3,2,1,0:T(8,128)} copy(f32[2,5,16,128]{3,2,1,0:T(8,128)} %shard_map.46) | data formatting | bytes 163840

commit v5 on v4

--- a/solution.py
+++ b/solution.py
@@ -21,7 +21,7 @@
 
 
 STEPS = sorted(((dx, dy, dc) for dx in range(4) for dy in range(4) for dc in range(2) if dx or dy or dc),
-               key=lambda s: -min(s[0], 4 - s[0]) - min(s[1], 4 - s[1]))
+               key=lambda s: (11 * (s[0] * 8 + s[1] * 2 + s[2])) % 32)
 
 
 def iota(shape, dim):
@@ -323,10 +323,11 @@
     send_plane(3, ps3, pr3)
     rhs3, rhs4 = xr[3].reshape(128, 256), xr[4].reshape(128, 256)
     ps4[...] = both_kinds(dot(lu[3], rhs3, 1, 0), dot(lu[4], rhs4, 1, 0))
+    send_plane(4, ps4, pr4)
     ps5[...] = both_kinds(dot(lv[3], rhs3, 1, 0), dot(lv[4], rhs4, 1, 0))
 
     arrived(1, pr1, (1,))
-    arrived(2, pr2, (2, 5), (4, ps4, pr4))
+    arrived(2, pr2, (2, 5), (5, ps5, pr5))
     extras_b = halves(jnp.concatenate([ab[5, EXTRA[j]] for j in (0, 1, 2)], axis=0))
 
     def gram_b(k, carry):
@@ -404,7 +405,7 @@
 
         return carry
 
-    arrived(3, pr3, (6,), (5, ps5, pr5))
+    arrived(3, pr3, (6,))
     extras_c = halves(jnp.concatenate([ab[6, EXTRA[j]] for j in (3, 4)], axis=0))
 
     def gram_left(kk, carry):
@@ -500,7 +501,7 @@
         out_specs=vmem,
         scratch_shapes=scratch,
         compiler_params=pltpu.CompilerParams(
-            collective_id=0, has_side_effects=True, vmem_limit_bytes=60 * 1024 * 1024),
+            collective_id=0, has_side_effects=True, vmem_limit_bytes=54784 * 1024),
     )(lon_count, wave_order, wave_order, field.reshape(LEV, LONS), legendre)
 
 

time: 73.1 us -> 71.5 us (0.978); the launches traced: 71.9 us -> 71.3 us
    unnamed x1 -> x3, local copies, waits for them, and re-layouts: 1.53 us -> 1.32 us
where the time goes in v5:
time: 71.5 us; the launch traced here: 71.3 us
  Pallas kernels  69.3 us (97%)
  local copies, waits for them, and re-layouts  1.32 us (2%)
    pallas_call x1, Pallas kernels, per_device(): pl.pallas_call(kernel, out_shape=jax.ShapeDtypeStruct((2, 5, 16, 128), F3...  69.3 us

profile of v5, /device:TPU:1, one launch (start us, length us, event | category | flops | bytes accessed | tf_op | source)
XLA Modules:
  0.0 71.3 jit_solution(14817427511827637356)
XLA Ops:
  0.7 0.0 copy-start
  0.7 0.7 copy-done
  1.3 69.3 %shard_map.46 = f32[2,5,16,128]{3,2,1,0:T(8,128)S(1)} custom-call(s32[1]{0:T(128)S(6)} %copy.6.count_ref, s32[640]{0:T(1024)S(1)} %copy-done, s32[640]{0:T(1024)S(1)} %copy-done, bf16[128,2688]{1,0:T(8,128)(2,1)} %bitcast.1, bf16[10,64,640]{2,1,0:T(8,128)(2,1)} %leg_ref.1), custom_call_target="tpu_custom_call" | custom-call | tf_op jit(solution)/shard_map/pallas_call | solution.py:497
  70.7 0.6 copy.7
Async XLA Ops:
  0.7 0.7 copy-start

commit v6 on v5

--- a/solution.py
+++ b/solution.py
@@ -308,14 +308,6 @@
             acc[k, 0] += near
             acc[k, 1] += far
 
-    arrived(0, pr0, (0,))
-
-    def gram_a(k, carry):
-        gram(k, [ab[0, k]], [ab[0, 8 + k]], (0,), True)
-        return carry
-
-    lax.fori_loop(0, 8, gram_a, 0)
-
     rows_along_z(3, zr3)
     gather(3, zr3, 0)
     gather(4, zr3, 16)
@@ -325,6 +317,14 @@
     ps4[...] = both_kinds(dot(lu[3], rhs3, 1, 0), dot(lu[4], rhs4, 1, 0))
     send_plane(4, ps4, pr4)
     ps5[...] = both_kinds(dot(lv[3], rhs3, 1, 0), dot(lv[4], rhs4, 1, 0))
+
+    arrived(0, pr0, (0,))
+
+    def gram_a(k, carry):
+        gram(k, [ab[0, k]], [ab[0, 8 + k]], (0,), True)
+        return carry
+
+    lax.fori_loop(0, 8, gram_a, 0)
 
     arrived(1, pr1, (1,))
     arrived(2, pr2, (2, 5), (5, ps5, pr5))

time: 71.5 us -> 71.4 us (level)
  no operation moved by 1% of the time
where the time goes in v6:
time: 71.4 us; the launch traced here: 71.2 us
  Pallas kernels  69.2 us (97%)
  local copies, waits for them, and re-layouts  1.32 us (2%)
    pallas_call x1, Pallas kernels, per_device(): pl.pallas_call(kernel, out_shape=jax.ShapeDtypeStruct((2, 5, 16, 128), F3...  69.2 us

profile of v6, /device:TPU:1, one launch (start us, length us, event | category | flops | bytes accessed | tf_op | source)
XLA Modules:
  0.0 71.2 jit_solution(1612369282464835609)
XLA Ops:
  0.7 0.0 copy-start
  0.7 0.7 copy-done
  1.3 69.2 %shard_map.46 = f32[2,5,16,128]{3,2,1,0:T(8,128)S(1)} custom-call(s32[1]{0:T(128)S(6)} %copy.6.count_ref, s32[640]{0:T(1024)S(1)} %copy-done, s32[640]{0:T(1024)S(1)} %copy-done, bf16[128,2688]{1,0:T(8,128)(2,1)} %bitcast.1, bf16[10,64,640]{2,1,0:T(8,128)(2,1)} %leg_ref.1), custom_call_target="tpu_custom_call" | custom-call | tf_op jit(solution)/shard_map/pallas_call | solution.py:497
  70.6 0.6 copy.7
Async XLA Ops:
  0.7 0.7 copy-start
